TPU v7x, 32 devices: a whole 2x2x4 slice. The times are simulated.
32 devices in a mesh: groups: 2 (over x), pencil: 16 (over z, y, core).
Axes of the slice: x: 2, y: 2, z: 4, core: 2. Of those that a mesh axis runs over, the one named last changes fastest.
Arguments:
- krylov_vector: bfloat16 [10, 512, 256, 128], P('groups', 'pencil'), parts along dimension 0, may hold values from -6 to 6
- base_wave: bfloat16 [10, 256, 512], P('groups', 'pencil'), parts along dimension 0, may hold values from -3 to 3
- radial_inverse: bfloat16 [258, 64, 64], P('groups'), parts along dimension 0, may hold values from -0.5 to 1.15
- step_counts: int32 [10], P('groups'), parts along dimension 0, may hold values from 1 to 3, as said below
- azimuth_shift: int32 [2], P('groups'), parts along dimension 0, may hold values from 0 to 255
- phase_tangent: bfloat16 [1024, 256, 128], P(('groups', 'pencil')), parts along dimension 0, may hold values from -1 to 1
Outputs:
- shooting: float32 [10, 512, 256, 128], P('groups', 'pencil'), parts along dimension 0
- phase_value: float32 [2], P('groups'), parts along dimension 0
There are 2 independent parts, one for each index of `groups`. A program takes and returns all parts, laid end to end along the dimension named above; each array names one. Nothing has to cross between parts.
Inputs may be any that keep to these rules, and one draw needn't show every extreme that they name: `step_counts`: some segment takes exactly 3 steps.
All inputs are finite; a program needn't handle non-finite values.
Results may differ from a plain program's by a relative error of at most 0.006.
Values may be sent and summed in bfloat16 or wider, within the bound.
A program may use at most 192 MiB of HBM per device.

v0:
```python
import jax
import jax.numpy as jnp
from jax import lax
from jax.sharding import PartitionSpec as P

NSTEP = 3


viscosity = 2e-06
step_size = 0.4


def fourier_table(length):
    points = jnp.arange(length, dtype=jnp.int32)
    columns = jnp.arange(length, dtype=jnp.int32)
    wave_numbers = (columns + 1) // 2
    phase_index = points[:, None] * wave_numbers[None, :] % length
    angles = phase_index.astype(jnp.float32) * (2.0 * jnp.pi / length)
    cosine_col = (columns % 2 == 1) | (columns == 0)
    edge_col = (columns == 0) | (columns == length - 1)
    scales = jnp.where(
        edge_col, 1.0 / jnp.sqrt(jnp.float32(length)), jnp.sqrt(jnp.float32(2.0 / length))
    )
    values = jnp.where(cosine_col[None, :], jnp.cos(angles), jnp.sin(angles))
    return values * scales[None, :]


def damping(axial_index, azimuth_count):
    waves_axial = (axial_index + 1) // 2
    waves_azimuth = (jnp.arange(azimuth_count, dtype=jnp.int32) + 1) // 2
    squared_sum = (
        waves_axial[:, None] * waves_axial[:, None]
        + waves_azimuth[None, :] * waves_azimuth[None, :]
    )
    return 1.0 / (1.0 + viscosity * squared_sum.astype(jnp.float32))


def expand_radial(radial_table, azimuth_count):
    half_count = azimuth_count // 2
    return jnp.concatenate(
        [
            radial_table[:1],
            jnp.repeat(radial_table[1:half_count], 2, axis=0),
            radial_table[half_count : half_count + 1],
        ],
        axis=0,
    )


def body(krylov_vector, base_wave, radial_inverse, step_counts, azimuth_shift, phase_tangent):
    segments, local_z, azimuths, channels = krylov_vector.shape
    radial_size = radial_inverse.shape[1]
    batch_count = channels // radial_size
    total_z = local_z * lax.axis_size("pencil")
    table_azimuth = fourier_table(azimuths).astype(jnp.bfloat16)
    table_axial = fourier_table(total_z).astype(jnp.bfloat16)
    axial_index = lax.axis_index("pencil") * local_z + jnp.arange(local_z, dtype=jnp.int32)
    damping_factor = damping(axial_index, azimuths)[None, :, :, None, None]
    radial_full = expand_radial(radial_inverse, azimuths)
    base_planes = jnp.swapaxes(base_wave, 1, 2)[..., None]
    current_state = krylov_vector
    for step_index in range(NSTEP):
        physical_m = jnp.einsum(
            "szmr,pm->szpr", current_state, table_azimuth, preferred_element_type=jnp.float32
        ).astype(jnp.bfloat16)
        arrived = lax.all_to_all(physical_m, "pencil", split_axis=2, concat_axis=1, tiled=True)
        physical = jnp.einsum(
            "szpr,xz->sxpr", arrived, table_axial, preferred_element_type=jnp.float32
        )
        product = (physical * base_planes.astype(jnp.float32)).astype(jnp.bfloat16)
        returned = jnp.einsum(
            "sxpr,xz->szpr", product, table_axial, preferred_element_type=jnp.float32
        ).astype(jnp.bfloat16)
        arrived_back = lax.all_to_all(returned, "pencil", split_axis=1, concat_axis=2, tiled=True)
        tendency = jnp.einsum(
            "szpr,pm->szmr", arrived_back, table_azimuth, preferred_element_type=jnp.float32
        )
        updated = (current_state.astype(jnp.float32) + step_size * tendency).astype(jnp.bfloat16)
        shaped = updated.reshape(
            current_state.shape[0], local_z, azimuths, batch_count, radial_size
        )
        applied = jnp.einsum(
            "szmkr,mor->szmko", shaped, radial_full, preferred_element_type=jnp.float32
        )
        advanced = (applied * damping_factor).reshape(current_state.shape).astype(jnp.bfloat16)
        current_state = jnp.where(
            (step_index < step_counts)[:, None, None, None], advanced, current_state
        )
    last_state = current_state[segments - 1]
    table_full = fourier_table(azimuths)
    physical_last = jnp.einsum(
        "zmr,pm->zpr", last_state.astype(jnp.float32), table_full, precision=lax.Precision.HIGHEST
    )
    rolled = jnp.roll(physical_last, azimuth_shift[0], axis=1)
    shifted = jnp.einsum("zpr,pm->zmr", rolled, table_full, precision=lax.Precision.HIGHEST)
    shooting = jnp.concatenate(
        [
            current_state[: segments - 1].astype(jnp.float32)
            - krylov_vector[1:].astype(jnp.float32),
            (shifted - krylov_vector[0].astype(jnp.float32))[None],
        ],
        axis=0,
    )
    local_phase = jnp.sum(phase_tangent.astype(jnp.float32) * krylov_vector[0].astype(jnp.float32))
    phase_value = lax.psum(local_phase, "pencil").reshape(1)
    return (shooting, phase_value)


def solution(mesh):
    return jax.shard_map(
        body,
        mesh=mesh,
        in_specs=(
            P("groups", "pencil", None, None),
            P("groups", "pencil", None),
            P("groups", None, None),
            P("groups"),
            P("groups"),
            P(("groups", "pencil"), None, None),
        ),
        out_specs=(P("groups", "pencil", None, None), P("groups")),
        check_vma=False,
    )
```

profile of v0, /device:TPU:18, one launch (start us, length us, event | category | flops | bytes accessed | tf_op | source)
XLA Modules:
  0.0 2102.3 jit_solution(2501819238237202779)
XLA Ops:
  0.7 10.7 convert_bitcast_fusion.5
  11.4 14.6 copy.167
  25.9 6.6 all-to-all-start
  32.6 227.3 %all-to-all-done = bf16[5,32,256,128]{3,1,0,2:T(8,128)(2,1)} async-done(((bf16[5,32,256,128]{3,1,0,2:T(8,128)(2,1)}), bf16[5,32,256,128]{3,1,0,2:T(8,128)(2,1)}, u32[]{:S(2)}, u32[]{:S(2)}) %all-to-all-start) | async-done | bytes 10485792 | tf_op jit(solution)/shard_map/all_to_all | solution.py:66
  259.9 18.5 copy.169
  278.4 19.5 fusion.199
  298.0 16.3 convert_bitcast_fusion.4
  314.3 14.6 copy.172
  328.9 5.0 all-to-all-start.1
  333.9 0.0 copy-start
  333.9 14.4 copy.165
  348.2 0.4 slice.23
  348.7 2.0 fusion.167
  350.6 1.7 copy.251
  352.3 1.7 copy.252
  354.0 3.3 copy.163
  357.3 0.1 add_divide_fusion
  357.4 0.1 copy.178
  357.5 0.5 broadcast_compare_fusion.2
  358.0 203.2 %all-to-all-done.1 = bf16[5,512,16,128]{3,2,0,1:T(8,128)(2,1)} async-done(((bf16[5,512,16,128]{3,2,0,1:T(8,128)(2,1)}), bf16[5,512,16,128]{3,2,0,1:T(8,128)(2,1)}, u32[]{:S(2)}, u32[]{:S(2)}) %all-to-all-start.1) | async-done | bytes 10485792 | tf_op jit(solution)/shard_map/all_to_all | solution.py:74
  561.2 11.2 copy.174
  572.4 18.5 fusion.7
  590.9 29.5 %copy.177 = bf16[5,32,256,2,64]{4,1,3,0,2:T(8,128)(2,1)} copy(bf16[5,32,256,2,64]{2,4,3,1,0:T(8,128)(2,1)} %bitcast.196) | data formatting | bytes 20971520 | tf_op jit(solution)/shard_map/reshape | solution.py:79
  620.4 3.2 broadcast_in_dim.107
  623.6 18.5 fusion.2
  642.2 24.6 %copy.179 = bf16[5,32,256,2,64]{2,4,3,1,0:T(8,128)(2,1)} copy(bf16[5,32,256,2,64]{4,1,3,0,2:T(8,128)(2,1)} %fusion.2) | data formatting | bytes 20971520 | tf_op jit(solution)/shard_map/convert_element_type | solution.py:85
  666.8 12.2 bitcast_select_fusion.2
  679.0 14.6 convert_bitcast_fusion.3
  693.6 14.7 copy.183
  708.3 232.9 %all_to_all.108 = bf16[5,32,256,128]{3,1,0,2:T(8,128)(2,1)} all-to-all(bf16[5,32,256,128]{3,1,0,2:T(8,128)(2,1)} %copy.183), channel_id=1, replica_groups=mesh['groups'=2,'pencil'=16] {'pencil'}, dimensions={2} | all-to-all | bytes 20971520 | tf_op jit(solution)/shard_map/all_to_all | solution.py:66
  941.3 18.5 copy.185
  959.8 19.5 fusion.195
  979.3 16.1 convert_bitcast_fusion.2
  995.4 14.7 copy.188
  1010.1 233.4 %all_to_all.109 = bf16[5,512,16,128]{3,2,0,1:T(8,128)(2,1)} all-to-all(bf16[5,512,16,128]{3,2,0,1:T(8,128)(2,1)} %copy.188), channel_id=1, replica_groups=mesh['groups'=2,'pencil'=16] {'pencil'}, dimensions={1} | all-to-all | bytes 20971520 | tf_op jit(solution)/shard_map/all_to_all | solution.py:74
  1243.5 11.2 copy.190
  1254.7 18.5 fusion.5
  1273.2 29.5 %copy.193 = bf16[5,32,256,2,64]{4,1,3,0,2:T(8,128)(2,1)} copy(bf16[5,32,256,2,64]{2,4,3,1,0:T(8,128)(2,1)} %bitcast.197) | data formatting | bytes 20971520 | tf_op jit(solution)/shard_map/reshape | solution.py:79
  1302.7 18.5 fusion.1
  1321.2 24.4 %copy.194 = bf16[5,32,256,2,64]{2,4,3,1,0:T(8,128)(2,1)} copy(bf16[5,32,256,2,64]{4,1,3,0,2:T(8,128)(2,1)} %fusion.1) | data formatting | bytes 20971520 | tf_op jit(solution)/shard_map/convert_element_type | solution.py:85
  1345.6 12.2 bitcast_select_fusion.1
  1357.9 15.1 convert_bitcast_fusion.1
  1373.0 14.7 copy.197
  1387.6 233.3 %all_to_all.110 = bf16[5,32,256,128]{3,1,0,2:T(8,128)(2,1)} all-to-all(bf16[5,32,256,128]{3,1,0,2:T(8,128)(2,1)} %copy.197), channel_id=1, replica_groups=mesh['groups'=2,'pencil'=16] {'pencil'}, dimensions={2} | all-to-all | bytes 20971520 | tf_op jit(solution)/shard_map/all_to_all | solution.py:66
  1620.9 18.5 copy.199
  1639.4 19.5 fusion.191
  1659.0 16.3 convert_bitcast_fusion
  1675.3 14.6 copy.202
  1689.9 5.2 all-to-all-start.5
  1695.1 3.3 copy.214
  1698.4 3.3 fusion.31
  1701.7 239.5 %psum.7 = f32[1]{0:T(128)} all-reduce(f32[1]{0:T(128)} %bitcast.71), channel_id=1, replica_groups=mesh['groups'=2,'pencil'=16] {'pencil'}, use_global_device_ids=true, to_apply=%region_1.2 | all-reduce | flops 1 | bytes 8 | tf_op jit(solution)/shard_map/psum | solution.py:105
  1941.9 0.0 all-to-all-done.5
  1941.9 11.2 copy.204
  1953.1 18.5 fusion.3
  1971.6 29.5 %copy.207 = bf16[5,32,256,2,64]{4,1,3,0,2:T(8,128)(2,1)} copy(bf16[5,32,256,2,64]{2,4,3,1,0:T(8,128)(2,1)} %bitcast.198) | data formatting | bytes 20971520 | tf_op jit(solution)/shard_map/reshape | solution.py:79
  2001.1 18.5 fusion
  2019.6 24.4 %copy.208 = bf16[5,32,256,2,64]{2,4,3,1,0:T(8,128)(2,1)} copy(bf16[5,32,256,2,64]{4,1,3,0,2:T(8,128)(2,1)} %fusion) | data formatting | bytes 20971520 | tf_op jit(solution)/shard_map/convert_element_type | solution.py:85
  2044.0 8.0 bitcast_select_fusion
  2052.0 5.7 convert_subtract_fusion
  2057.7 4.6 convolution_bitcast_fusion
  2062.4 10.1 fusion.30
  2072.5 7.4 pad_maximum_fusion
  2079.8 22.3 %copy.215 = f32[5,32,256,128]{3,2,1,0:T(8,128)} copy(f32[5,32,256,128]{2,3,1,0:T(8,128)} %pad_maximum_fusion) | data formatting | bytes 41943040
  (18 shorter events, 0.1 us)
Async XLA Ops:
  25.9 6.7 copy-start.1
  25.9 234.0 %all-to-all-start = ((bf16[5,32,256,128]{3,1,0,2:T(8,128)(2,1)}), bf16[5,32,256,128]{3,1,0,2:T(8,128)(2,1)}, u32[]{:S(2)}, u32[]{:S(2)}) async-start(bf16[5,32,256,128]{3,1,0,2:T(8,128)(2,1)} %copy.167), calls=%async_computation | async-start | bytes 20971520 | tf_op jit(solution)/shard_map/all_to_all | solution.py:66
  328.9 232.4 %all-to-all-start.1 = ((bf16[5,512,16,128]{3,2,0,1:T(8,128)(2,1)}), bf16[5,512,16,128]{3,2,0,1:T(8,128)(2,1)}, u32[]{:S(2)}, u32[]{:S(2)}) async-start(bf16[5,512,16,128]{3,2,0,1:T(8,128)(2,1)} %copy.172), calls=%async_computation.1 | async-start | bytes 20971520 | tf_op jit(solution)/shard_map/all_to_all | solution.py:74
  333.9 14.4 copy-start
  348.2 9.3 copy-start.4
  1321.2 24.4 %copy-start.3 = (pred[5]{0:T(512)(128)(4,1)S(1)}, pred[5]{0:T(512)(128)(4,1)}, u32[]{:S(2)}) copy-start(pred[5]{0:T(512)(128)(4,1)} %get-tuple-element.16) | copy-start | bytes 19
  1689.9 252.0 %all-to-all-start.5 = ((bf16[5,512,16,128]{3,2,0,1:T(8,128)(2,1)}), bf16[5,512,16,128]{3,2,0,1:T(8,128)(2,1)}, u32[]{:S(2)}, u32[]{:S(2)}) async-start(bf16[5,512,16,128]{3,2,0,1:T(8,128)(2,1)} %copy.202), calls=%async_computation.5 | async-start | bytes 20971520 | tf_op jit(solution)/shard_map/all_to_all | solution.py:74
  2019.6 24.4 %copy-start.2 = (pred[5]{0:T(512)(128)(4,1)S(1)}, pred[5]{0:T(512)(128)(4,1)}, u32[]{:S(2)}) copy-start(pred[5]{0:T(512)(128)(4,1)} %get-tuple-element.14) | copy-start | bytes 19
where the time goes:
time: 2120 us; the launch traced here: 2100 us
  blocking collectives  939 us (44%)
  waiting for transfers between devices  430 us (20%)
  local copies, waits for them, and re-layouts  391 us (18%)
  matrix products  274 us (13%)
  other arithmetic  49.5 us (2%)
    all_to_all x2, blocking collectives, body(): lax.all_to_all(physical_m, 'pencil', split_axis=2, concat_axis=1, tiled=T...  466 us
    psum x1, blocking collectives, body(): phase_value = lax.psum(local_phase, 'pencil').reshape(1)  239 us
    all_to_all x1, blocking collectives, body(): lax.all_to_all(returned, 'pencil', split_axis=1, concat_axis=2, tiled=True)  233 us
    all_to_all x1, waiting for transfers between devices, body(): lax.all_to_all(physical_m, 'pencil', split_axis=2, concat_axis=1, tiled=T...  227 us
    all_to_all x2, waiting for transfers between devices, body(): lax.all_to_all(returned, 'pencil', split_axis=1, concat_axis=2, tiled=True)  203 us
    reshape x3, local copies, waits for them, and re-layouts, body(): updated.reshape(current_state.shape[0], local_z, azimuths, batch_count, r...  88.6 us
    convert_element_type x3, local copies, waits for them, and re-layouts, body(): (applied * damping_factor).reshape(current_state.shape).astype(jnp.bfloat16)  73.4 us
    dot_general x3, matrix products, body(): jnp.einsum('szpr,xz->sxpr', arrived, table_axial, preferred_element_type=...  58.6 us
  transfers between devices with their start and end apart: 3, of which 2 were waited for; matrix products, arithmetic and copies ran while one was open for 1% of the time, Pallas kernels for 0%

commit v1 on v0

v1 whole, which is shorter than its diff:
```python
import functools
import jax
import jax.numpy as jnp
from jax import lax
from jax.experimental import pallas as pl
from jax.experimental.pallas import tpu as pltpu
from jax.sharding import PartitionSpec as P

NSTEP = 3


viscosity = 2e-06
step_size = 0.4


def fourier_table(length):
    points = jnp.arange(length, dtype=jnp.int32)
    columns = jnp.arange(length, dtype=jnp.int32)
    wave_numbers = (columns + 1) // 2
    phase_index = points[:, None] * wave_numbers[None, :] % length
    angles = phase_index.astype(jnp.float32) * (2.0 * jnp.pi / length)
    cosine_col = (columns % 2 == 1) | (columns == 0)
    edge_col = (columns == 0) | (columns == length - 1)
    scales = jnp.where(
        edge_col, 1.0 / jnp.sqrt(jnp.float32(length)), jnp.sqrt(jnp.float32(2.0 / length))
    )
    values = jnp.where(cosine_col[None, :], jnp.cos(angles), jnp.sin(angles))
    return values * scales[None, :]


def damping(axial_index, azimuth_count):
    waves_axial = (axial_index + 1) // 2
    waves_azimuth = (jnp.arange(azimuth_count, dtype=jnp.int32) + 1) // 2
    squared_sum = (
        waves_axial[:, None] * waves_axial[:, None]
        + waves_azimuth[None, :] * waves_azimuth[None, :]
    )
    return 1.0 / (1.0 + viscosity * squared_sum.astype(jnp.float32))


def expand_radial(radial_table, azimuth_count):
    half_count = azimuth_count // 2
    return jnp.concatenate(
        [
            radial_table[:1],
            jnp.repeat(radial_table[1:half_count], 2, axis=0),
            radial_table[half_count : half_count + 1],
        ],
        axis=0,
    )


def advance(state, base_plane, radial_full, table_azimuth, table_axial, damping_factor):
    local_z, azimuths, channels = state.shape
    radial_size = radial_full.shape[1]
    physical_m = jnp.einsum(
        "zmr,pm->pzr", state, table_azimuth, preferred_element_type=jnp.float32
    ).astype(jnp.bfloat16)
    arrived = lax.all_to_all(physical_m, "pencil", split_axis=0, concat_axis=1, tiled=True)
    physical = jnp.einsum("pzr,xz->pxr", arrived, table_axial, preferred_element_type=jnp.float32)
    product = (physical * base_plane.astype(jnp.float32)[..., None]).astype(jnp.bfloat16)
    returned = jnp.einsum(
        "pxr,xz->pzr", product, table_axial, preferred_element_type=jnp.float32
    ).astype(jnp.bfloat16)
    arrived_back = lax.all_to_all(returned, "pencil", split_axis=1, concat_axis=0, tiled=True)
    tendency = jnp.einsum(
        "pzr,pm->zmr", arrived_back, table_azimuth, preferred_element_type=jnp.float32
    )
    updated = (state.astype(jnp.float32) + step_size * tendency).astype(jnp.bfloat16)
    shaped = updated.reshape(local_z, azimuths, channels // radial_size, radial_size)
    applied = jnp.einsum(
        "zmkr,mor->zmko", shaped, radial_full, preferred_element_type=jnp.float32
    )
    return (applied * damping_factor[:, :, None, None]).reshape(state.shape).astype(jnp.bfloat16)


BLOCK = 16
VMEM_BYTES = 48 * 1024 * 1024


def swap_block(source, first, second):
    block = source[pl.ds(first, BLOCK), pl.ds(second, BLOCK), :].astype(jnp.float32)
    return jnp.swapaxes(block, 0, 1).astype(jnp.bfloat16)


def swap_all(source, target, rows, columns):
    def one(index, _):
        first = pl.multiple_of(index * BLOCK, BLOCK)
        for second in range(0, columns, BLOCK):
            target[pl.ds(second, BLOCK), pl.ds(first, BLOCK), :] = swap_block(source, first, second)
        return 0

    lax.fori_loop(0, rows // BLOCK, one, 0)


def analyse(state, table, spread, out, local_z, azimuths):
    def one(index, _):
        first = index * 4
        right = jnp.concatenate([state[first + j] for j in range(4)], axis=1)
        result = jnp.dot(table[...], right, preferred_element_type=jnp.float32)
        result = result.astype(jnp.bfloat16)
        for j in range(4):
            spread[first + j] = result[:, j * 128 : (j + 1) * 128]
        return 0

    lax.fori_loop(0, local_z // 4, one, 0)
    swap_all(spread, out, local_z, azimuths)


def start_kernel(state, table, out, spread):
    local_z, azimuths, _ = state.shape
    analyse(state, table, spread, out, local_z, azimuths)


def start_call(state, table_azimuth):
    local_z, azimuths, channels = state.shape
    vmem = pl.BlockSpec(memory_space=pltpu.VMEM)
    return pl.pallas_call(
        start_kernel,
        out_shape=jax.ShapeDtypeStruct((azimuths, local_z, channels), jnp.bfloat16),
        in_specs=[vmem, vmem],
        out_specs=vmem,
        scratch_shapes=[pltpu.VMEM(state.shape, jnp.bfloat16)],
        compiler_params=pltpu.CompilerParams(vmem_limit_bytes=VMEM_BYTES),
        cost_estimate=pl.CostEstimate(
            flops=2 * azimuths * state.size, bytes_accessed=6 * state.size, transcendentals=0
        ),
    )(state, table_azimuth)


def middle_kernel(arrived, base, table, table_t, out):
    pencils, count, local_z, channels = arrived.shape
    total_z = pencils * local_z
    right = jnp.concatenate(
        [arrived[:, j].reshape(total_z, channels) for j in range(count)], axis=1
    )
    physical = jnp.dot(table[...], right, preferred_element_type=jnp.float32)
    planes = jnp.concatenate(
        [jnp.broadcast_to(base[j], (channels, total_z)).T for j in range(count)], axis=1
    )
    product = (physical * planes).astype(jnp.bfloat16)
    back = jnp.dot(table_t[...], product, preferred_element_type=jnp.float32)
    back = back.astype(jnp.bfloat16)
    for j in range(count):
        out[:, j] = back[:, j * channels : (j + 1) * channels].reshape(pencils, local_z, channels)


def middle_call(arrived, base, table, table_t):
    pencils, points, local_z, channels = arrived.shape
    total_z = pencils * local_z
    count = 4
    block = pl.BlockSpec((pencils, count, local_z, channels), lambda p: (0, p, 0, 0))
    whole = pl.BlockSpec((total_z, total_z), lambda p: (0, 0))
    return pl.pallas_call(
        middle_kernel,
        grid=(points // count,),
        out_shape=jax.ShapeDtypeStruct(arrived.shape, jnp.bfloat16),
        in_specs=[block, pl.BlockSpec((count, 1, total_z), lambda p: (p, 0, 0)), whole, whole],
        out_specs=block,
        compiler_params=pltpu.CompilerParams(vmem_limit_bytes=VMEM_BYTES),
        cost_estimate=pl.CostEstimate(
            flops=4 * total_z * arrived.size, bytes_accessed=4 * arrived.size, transcendentals=0
        ),
    )(arrived, base, table, table_t)


def finish_kernel(
    last, active, back, state, radial, waves_squared, table, table_t, new_state, *rest
):
    out = None if last else rest[0]
    spread, by_mode = rest[-2:]
    local_z, azimuths, channels = state.shape
    half = azimuths // 2
    swap_all(back, spread, azimuths, local_z)

    def tendency(index, _):
        first = index * 4
        right = jnp.concatenate([spread[first + j] for j in range(4)], axis=1)
        result = jnp.dot(table_t[...], right, preferred_element_type=jnp.float32)
        for j in range(4):
            updated = state[first + j].astype(jnp.float32) + step_size * result[
                :, j * channels : (j + 1) * channels
            ]
            spread[first + j] = updated.astype(jnp.bfloat16)
        return 0

    lax.fori_loop(0, local_z // 4, tendency, 0)
    swap_all(spread, by_mode, local_z, azimuths)

    def radial_step(wave, first, count):
        left = by_mode[pl.ds(first, count)].reshape(count * local_z, channels)
        applied = jnp.dot(left, radial[wave], preferred_element_type=jnp.float32)
        wave_f = jnp.asarray(wave, jnp.int32).astype(jnp.float32)
        factor = 1.0 / (1.0 + viscosity * (waves_squared[...] + wave_f * wave_f))
        result = applied.reshape(count, local_z, channels) * factor[None]
        by_mode[pl.ds(first, count)] = result.astype(jnp.bfloat16)

    radial_step(0, 0, 1)
    radial_step(half, azimuths - 1, 1)
    group = 8
    loops = (half - 1) // group

    def several(index, _):
        for j in range(group):
            wave = 1 + index * group + j
            radial_step(wave, 2 * wave - 1, 2)
        return 0

    lax.fori_loop(0, loops, several, 0)
    for wave in range(1 + loops * group, half):
        radial_step(wave, 2 * wave - 1, 2)
    swap_all(by_mode, spread, azimuths, local_z)
    keep = active[0] > 0

    def choose(index, _):
        new_state[index] = jnp.where(keep, spread[index], state[index])
        return 0

    lax.fori_loop(0, local_z, choose, 0)
    if not last:
        analyse(new_state, table, spread, out, local_z, azimuths)


def finish_call(last, active, back, state, radial, waves_squared, table, table_t):
    local_z, azimuths, channels = state.shape
    vmem = pl.BlockSpec(memory_space=pltpu.VMEM)
    state_shape = jax.ShapeDtypeStruct(state.shape, jnp.bfloat16)
    out_shape = jax.ShapeDtypeStruct(back.shape, jnp.bfloat16)
    shapes = [state_shape] if last else [state_shape, out_shape]
    return pl.pallas_call(
        functools.partial(finish_kernel, last),
        out_shape=shapes,
        in_specs=[pl.BlockSpec(memory_space=pltpu.SMEM)] + [vmem] * 6,
        out_specs=[vmem] * len(shapes),
        scratch_shapes=[
            pltpu.VMEM(state.shape, jnp.bfloat16),
            pltpu.VMEM(back.shape, jnp.bfloat16),
        ],
        compiler_params=pltpu.CompilerParams(vmem_limit_bytes=VMEM_BYTES),
        cost_estimate=pl.CostEstimate(
            flops=4 * azimuths * state.size * 4, bytes_accessed=8 * state.size, transcendentals=0
        ),
    )(active, back, state, radial, waves_squared, table, table_t)


def run_kernels(states, base_wave, radial_inverse, step_counts, waves_axial, tables):
    segments = len(states)
    local_z, azimuths, channels = states[0].shape
    points = base_wave.shape[1]
    pencils = azimuths // points
    table_azimuth, table_axial = tables
    transposed = jnp.swapaxes(radial_inverse, 1, 2)
    blank = jnp.zeros_like(transposed)
    radial = transposed
    if channels != radial.shape[1]:
        radial = jnp.concatenate(
            [
                jnp.concatenate([transposed, blank], axis=2),
                jnp.concatenate([blank, transposed], axis=2),
            ],
            axis=1,
        )
    waves_f = waves_axial.astype(jnp.float32)
    waves_squared = jnp.broadcast_to((waves_f * waves_f)[:, None], (local_z, channels))
    base = base_wave.astype(jnp.float32)[:, :, None, :]
    shape = (pencils, points, local_z, channels)
    sent = [start_call(states[s], table_azimuth) for s in range(segments)]
    for step_index in range(NSTEP):
        last = step_index == NSTEP - 1
        for s in range(segments):
            arrived = lax.all_to_all(
                sent[s].reshape(shape), "pencil", split_axis=0, concat_axis=0, tiled=True
            )
            product = middle_call(arrived, base[s], table_axial, table_axial.T)
            back = lax.all_to_all(product, "pencil", split_axis=0, concat_axis=0, tiled=True)
            active = (step_index < step_counts[s : s + 1]).astype(jnp.int32)
            results = finish_call(
                last,
                active,
                back.reshape(azimuths, local_z, channels),
                states[s],
                radial,
                waves_squared,
                table_azimuth,
                table_azimuth.T,
            )
            states[s] = results[0]
            if not last:
                sent[s] = results[1]
    return states


def body(krylov_vector, base_wave, radial_inverse, step_counts, azimuth_shift, phase_tangent):
    segments, local_z, azimuths, channels = krylov_vector.shape
    total_z = local_z * lax.axis_size("pencil")
    table_azimuth = fourier_table(azimuths).astype(jnp.bfloat16)
    table_axial = fourier_table(total_z).astype(jnp.bfloat16)
    axial_index = lax.axis_index("pencil") * local_z + jnp.arange(local_z, dtype=jnp.int32)
    damping_factor = damping(axial_index, azimuths)
    radial_full = expand_radial(radial_inverse, azimuths)
    states = [krylov_vector[s] for s in range(segments)]
    fits = (
        local_z % BLOCK == 0
        and azimuths % BLOCK == 0
        and base_wave.shape[1] % 4 == 0
        and channels == 128
        and channels == 2 * radial_inverse.shape[1]
    )
    if fits:
        states = run_kernels(
            states,
            base_wave,
            radial_inverse,
            step_counts,
            (axial_index + 1) // 2,
            (table_azimuth, table_axial),
        )
    else:
        for step_index in range(NSTEP):
            for s in range(segments):
                advanced = advance(
                    states[s], base_wave[s], radial_full, table_azimuth, table_axial, damping_factor
                )
                states[s] = (
                    advanced
                    if step_index == 0
                    else jnp.where(step_index < step_counts[s], advanced, states[s])
                )
    table_full = fourier_table(azimuths)
    physical_last = jnp.einsum(
        "zmr,pm->zpr",
        states[-1].astype(jnp.float32),
        table_full,
        precision=lax.Precision.HIGHEST,
    )
    rolled = jnp.roll(physical_last, azimuth_shift[0], axis=1)
    shifted = jnp.einsum("zpr,pm->zmr", rolled, table_full, precision=lax.Precision.HIGHEST)
    shooting = jnp.stack(
        [
            states[s].astype(jnp.float32) - krylov_vector[s + 1].astype(jnp.float32)
            for s in range(segments - 1)
        ]
        + [shifted - krylov_vector[0].astype(jnp.float32)],
        axis=0,
    )
    local_phase = jnp.sum(phase_tangent.astype(jnp.float32) * krylov_vector[0].astype(jnp.float32))
    phase_value = lax.psum(local_phase, "pencil").reshape(1)
    return (shooting, phase_value)


def solution(mesh):
    return jax.shard_map(
        body,
        mesh=mesh,
        in_specs=(
            P("groups", "pencil", None, None),
            P("groups", "pencil", None),
            P("groups", None, None),
            P("groups"),
            P("groups"),
            P(("groups", "pencil"), None, None),
        ),
        out_specs=(P("groups", "pencil", None, None), P("groups")),
        check_vma=False,
    )
```

time: 2120 us -> 1780 us (0.84)
  blocking collectives: 939 us -> 62.2 us
  waiting for transfers between devices: 430 us -> 945 us
  Pallas kernels: 0 us -> 473 us
  local copies, waits for them, and re-layouts: 391 us -> 79.9 us
  matrix products: 274 us -> 13.8 us
  starting transfers between devices: 16.9 us -> 143 us
    all_to_all x3 -> x0, blocking collectives: 700 us -> none  [the longest x2 466 us: body(): lax.all_to_all(physical_m, 'pencil', split_axis=2, concat_axis=1, tiled=T...]
    all_to_all x3 -> x30, waiting for transfers between devices: 430 us -> 945 us  [the longest x15 522 us: run_kernels(): lax.all_to_all(product, 'pencil', split_axis=0, concat_axis=0, tiled=True)]
    pallas_call x0 -> x35, Pallas kernels: none -> 473 us  [the longest x15 391 us: finish_call(): pl.pallas_call(functools.partial(finish_kernel, last), out_shape=shapes,...]
    dot_general x16 -> x1, matrix products: 264 us -> 4.4 us  [body(): jnp.einsum('zmr,pm->zpr', states[-1].astype(jnp.float32), table_full, pre...]
    psum x1, blocking collectives: 239 us -> 62.2 us  [body(): phase_value = lax.psum(local_phase, 'pencil').reshape(1)]
    convert_element_type x9 -> x0, local copies, waits for them, and re-layouts: 161 us -> none  [the longest x3 73.4 us: body(): (applied * damping_factor).reshape(current_state.shape).astype(jnp.bfloat16)]
    all_to_all x3 -> x30, starting transfers between devices: 16.9 us -> 143 us  [the longest x15 72.7 us: run_kernels(): lax.all_to_all(sent[s].reshape(shape), 'pencil', split_axis=0, concat_axi...]
    all_to_all x6 -> x0, local copies, waits for them, and re-layouts: 89.1 us -> none  [the longest x3 55.6 us: body(): lax.all_to_all(physical_m, 'pencil', split_axis=2, concat_axis=1, tiled=T...]
  transfers between devices with their start and end apart: 3 -> 30, of which waited for: 2 -> 29; matrix products, arithmetic and copies ran while one was open for 1% -> 2% of each run, Pallas kernels for 0% -> 25%
where the time goes in v1:
time: 1780 us; the launch traced here: 1770 us
  waiting for transfers between devices  945 us (53%)
  Pallas kernels  473 us (27%)
  starting transfers between devices  143 us (8%)
  local copies, waits for them, and re-layouts  79.9 us (4%)
  blocking collectives  62.2 us (3%)
  other arithmetic  38 us (2%)
    all_to_all x15, waiting for transfers between devices, run_kernels(): lax.all_to_all(product, 'pencil', split_axis=0, concat_axis=0, tiled=True)  522 us
    all_to_all x15, waiting for transfers between devices, run_kernels(): lax.all_to_all(sent[s].reshape(shape), 'pencil', split_axis=0, concat_axi...  423 us
    pallas_call x15, Pallas kernels, finish_call(): pl.pallas_call(functools.partial(finish_kernel, last), out_shape=shapes,...  391 us
    all_to_all x15, starting transfers between devices, run_kernels(): lax.all_to_all(sent[s].reshape(shape), 'pencil', split_axis=0, concat_axi...  72.7 us
    unnamed x121, local copies, waits for them, and re-layouts  72.1 us
    all_to_all x15, starting transfers between devices, run_kernels(): lax.all_to_all(product, 'pencil', split_axis=0, concat_axis=0, tiled=True)  70.6 us
    pallas_call x15, Pallas kernels, middle_call(): pl.pallas_call(middle_kernel, grid=(points // count,), out_shape=jax.Shap...  68.1 us
    psum x1, blocking collectives, body(): phase_value = lax.psum(local_phase, 'pencil').reshape(1)  62.2 us
  transfers between devices with their start and end apart: 30, of which 29 were waited for; matrix products, arithmetic and copies ran while one was open for 2% of the time, Pallas kernels for 25%

profile of v1, /device:TPU:18, one launch (start us, length us, event | category | flops | bytes accessed | tf_op | source)
XLA Modules:
  0.0 1766.6 jit_solution(8683093231558332033)
XLA Ops:
  0.7 7.0 slice_bitcast_fusion
  14.2 6.2 all-to-all-start.24
  26.1 42.1 %all-to-all-done.24.arrived = bf16[16,16,32,128]{3,2,1,0:T(8,128)(2,1)} async-done(((bf16[16,16,32,128]{3,2,1,0:T(8,128)(2,1)}), bf16[16,16,32,128]{3,2,1,0:T(8,128)(2,1)}, u32[]{:S(2)}, u32[]{:S(2)}) %all-to-all-start.24) | async-done | bytes 2097184 | tf_op jit(solution)/shard_map/all_to_all | solution.py:271
  68.2 4.7 all-to-all-start.18
  78.5 42.1 %all-to-all-done.18.arrived = bf16[16,16,32,128]{3,2,1,0:T(8,128)(2,1)} async-done(((bf16[16,16,32,128]{3,2,1,0:T(8,128)(2,1)}), bf16[16,16,32,128]{3,2,1,0:T(8,128)(2,1)}, u32[]{:S(2)}, u32[]{:S(2)}) %all-to-all-start.18) | async-done | bytes 2097184 | tf_op jit(solution)/shard_map/all_to_all | solution.py:271
  131.0 42.1 %all-to-all-done.12.arrived = bf16[16,16,32,128]{3,2,1,0:T(8,128)(2,1)} async-done(((bf16[16,16,32,128]{3,2,1,0:T(8,128)(2,1)}), bf16[16,16,32,128]{3,2,1,0:T(8,128)(2,1)}, u32[]{:S(2)}, u32[]{:S(2)}) %all-to-all-start.12) | async-done | bytes 2097184 | tf_op jit(solution)/shard_map/all_to_all | solution.py:271
  181.8 43.7 %all-to-all-done.6.arrived = bf16[16,16,32,128]{3,2,1,0:T(8,128)(2,1)} async-done(((bf16[16,16,32,128]{3,2,1,0:T(8,128)(2,1)}), bf16[16,16,32,128]{3,2,1,0:T(8,128)(2,1)}, u32[]{:S(2)}, u32[]{:S(2)}) %all-to-all-start.6) | async-done | bytes 2097184 | tf_op jit(solution)/shard_map/all_to_all | solution.py:271
  225.5 4.8 all-to-all-start
  230.5 9.1 multiply_convert_fusion
  246.4 31.6 %all-to-all-done.arrived = bf16[16,16,32,128]{3,2,1,0:T(8,128)(2,1)S(1)} async-done(((bf16[16,16,32,128]{3,2,1,0:T(8,128)(2,1)}), bf16[16,16,32,128]{3,2,1,0:T(8,128)(2,1)S(1)}, u32[]{:S(2)}, u32[]{:S(2)}) %all-to-all-start) | async-done | bytes 2097184 | tf_op jit(solution)/shard_map/all_to_all | solution.py:271
  277.9 4.7 all-to-all-start.25
  289.6 40.8 %all-to-all-done.25 = bf16[16,16,32,128]{3,2,1,0:T(8,128)(2,1)} async-done(((bf16[16,16,32,128]{3,2,1,0:T(8,128)(2,1)}), bf16[16,16,32,128]{3,2,1,0:T(8,128)(2,1)}, u32[]{:S(2)}, u32[]{:S(2)}) %all-to-all-start.25) | async-done | bytes 2097184 | tf_op jit(solution)/shard_map/all_to_all | solution.py:275
  342.0 40.8 %all-to-all-done.19 = bf16[16,16,32,128]{3,2,1,0:T(8,128)(2,1)} async-done(((bf16[16,16,32,128]{3,2,1,0:T(8,128)(2,1)}), bf16[16,16,32,128]{3,2,1,0:T(8,128)(2,1)}, u32[]{:S(2)}, u32[]{:S(2)}) %all-to-all-start.19) | async-done | bytes 2097184 | tf_op jit(solution)/shard_map/all_to_all | solution.py:275
  382.8 5.0 all-to-all-start.13
  394.8 40.6 %all-to-all-done.13 = bf16[16,16,32,128]{3,2,1,0:T(8,128)(2,1)} async-done(((bf16[16,16,32,128]{3,2,1,0:T(8,128)(2,1)}), bf16[16,16,32,128]{3,2,1,0:T(8,128)(2,1)}, u32[]{:S(2)}, u32[]{:S(2)}) %all-to-all-start.13) | async-done | bytes 2097184 | tf_op jit(solution)/shard_map/all_to_all | solution.py:275
  445.9 42.0 %all-to-all-done.7 = bf16[16,16,32,128]{3,2,1,0:T(8,128)(2,1)} async-done(((bf16[16,16,32,128]{3,2,1,0:T(8,128)(2,1)}), bf16[16,16,32,128]{3,2,1,0:T(8,128)(2,1)}, u32[]{:S(2)}, u32[]{:S(2)}) %all-to-all-start.7) | async-done | bytes 2097184 | tf_op jit(solution)/shard_map/all_to_all | solution.py:275
  498.2 4.9 fusion.2.radial
  503.2 27.0 %shard_map.107 = (bf16[32,256,128]{2,1,0:T(8,128)(2,1)S(1)}, bf16[256,32,128]{2,1,0:T(8,128)(2,1)S(1)}) custom-call(s32[1]{0:T(128)S(6)} %convert_element_type.390.active, bf16[256,32,128]{2,1,0:T(8,128)(2,1)} %bitcast.42.back, bf16[32,256,128]{2,1,0:T(8,128)(2,1)} %copy-done.4, bf16[129,128,128]{2,1,0:T(8,128)(2,1)} %fusion.2.radial, ...), custom_call_target="tpu_custom_call" | custom-call | flops 4294967296 | bytes 8388608 | tf_op jit(solution)/shard_map/pallas_call | solution.py:230
  532.9 7.4 all-to-all-done.1
  545.6 27.0 %shard_map.100 = (bf16[32,256,128]{2,1,0:T(8,128)(2,1)S(1)}, bf16[256,32,128]{2,1,0:T(8,128)(2,1)S(1)}) custom-call(s32[1]{0:T(128)S(6)} %convert_element_type.385.active, bf16[256,32,128]{2,1,0:T(8,128)(2,1)} %bitcast.31.back, bf16[32,256,128]{2,1,0:T(8,128)(2,1)} %get-tuple-element.46.state, bf16[129,128,128]{2,1,0:T(8,128)(2,1)} %fusion.2.radial, ...), custom_call_target="tpu_custom_call" | custom-call | flops 4294967296 | bytes 8388608 | tf_op jit(solution)/shard_map/pallas_call | solution.py:230
  575.3 17.4 all-to-all-done.26.arrived
  597.9 27.0 %shard_map.93 = (bf16[32,256,128]{2,1,0:T(8,128)(2,1)S(1)}, bf16[256,32,128]{2,1,0:T(8,128)(2,1)S(1)}) custom-call(s32[1]{0:T(128)S(6)} %convert_element_type.380.active, bf16[256,32,128]{2,1,0:T(8,128)(2,1)} %bitcast.22.back, bf16[32,256,128]{2,1,0:T(8,128)(2,1)} %get-tuple-element.43.state, bf16[129,128,128]{2,1,0:T(8,128)(2,1)} %fusion.2.radial, ...), custom_call_target="tpu_custom_call" | custom-call | flops 4294967296 | bytes 8388608 | tf_op jit(solution)/shard_map/pallas_call | solution.py:230
  627.6 17.5 all-to-all-done.20.arrived
  645.1 4.7 all-to-all-start.14
  650.4 27.0 %shard_map.86 = (bf16[32,256,128]{2,1,0:T(8,128)(2,1)S(1)}, bf16[256,32,128]{2,1,0:T(8,128)(2,1)S(1)}) custom-call(s32[1]{0:T(128)S(6)} %convert_element_type.375.active, bf16[256,32,128]{2,1,0:T(8,128)(2,1)} %bitcast.13.back, bf16[32,256,128]{2,1,0:T(8,128)(2,1)} %get-tuple-element.44.state, bf16[129,128,128]{2,1,0:T(8,128)(2,1)} %fusion.2.radial, ...), custom_call_target="tpu_custom_call" | custom-call | flops 4294967296 | bytes 8388608 | tf_op jit(solution)/shard_map/pallas_call | solution.py:230
  680.1 17.4 all-to-all-done.14.arrived
  697.5 5.2 all-to-all-start.8
  703.4 27.0 %shard_map.79 = (bf16[32,256,128]{2,1,0:T(8,128)(2,1)S(1)}, bf16[256,32,128]{2,1,0:T(8,128)(2,1)S(1)}) custom-call(s32[1]{0:T(128)S(6)} %convert_element_type.360.active, bf16[256,32,128]{2,1,0:T(8,128)(2,1)} %bitcast.3.back, bf16[32,256,128]{2,1,0:T(8,128)(2,1)} %copy-done, bf16[129,128,128]{2,1,0:T(8,128)(2,1)} %fusion.2.radial, ...), custom_call_target="tpu_custom_call" | custom-call | flops 4294967296 | bytes 8388608 | tf_op jit(solution)/shard_map/pallas_call | solution.py:230
  733.1 17.3 all-to-all-done.8.arrived
  760.8 41.9 %all-to-all-done.2.arrived = bf16[16,16,32,128]{3,2,1,0:T(8,128)(2,1)} async-done(((bf16[16,16,32,128]{3,2,1,0:T(8,128)(2,1)}), bf16[16,16,32,128]{3,2,1,0:T(8,128)(2,1)}, u32[]{:S(2)}, u32[]{:S(2)}) %all-to-all-start.2) | async-done | bytes 2097184 | tf_op jit(solution)/shard_map/all_to_all | solution.py:271
  807.4 5.6 shard_map.101
  813.0 42.2 %all-to-all-done.27 = bf16[16,16,32,128]{3,2,1,0:T(8,128)(2,1)} async-done(((bf16[16,16,32,128]{3,2,1,0:T(8,128)(2,1)}), bf16[16,16,32,128]{3,2,1,0:T(8,128)(2,1)}, u32[]{:S(2)}, u32[]{:S(2)}) %all-to-all-start.27) | async-done | bytes 2097184 | tf_op jit(solution)/shard_map/all_to_all | solution.py:275
  859.9 5.5 shard_map.94
  865.4 42.2 %all-to-all-done.21 = bf16[16,16,32,128]{3,2,1,0:T(8,128)(2,1)} async-done(((bf16[16,16,32,128]{3,2,1,0:T(8,128)(2,1)}), bf16[16,16,32,128]{3,2,1,0:T(8,128)(2,1)}, u32[]{:S(2)}, u32[]{:S(2)}) %all-to-all-start.21) | async-done | bytes 2097184 | tf_op jit(solution)/shard_map/all_to_all | solution.py:275
  907.6 4.7 all-to-all-start.15
  912.3 5.5 shard_map.87
  917.9 42.2 %all-to-all-done.15 = bf16[16,16,32,128]{3,2,1,0:T(8,128)(2,1)} async-done(((bf16[16,16,32,128]{3,2,1,0:T(8,128)(2,1)}), bf16[16,16,32,128]{3,2,1,0:T(8,128)(2,1)}, u32[]{:S(2)}, u32[]{:S(2)}) %all-to-all-start.15) | async-done | bytes 2097184 | tf_op jit(solution)/shard_map/all_to_all | solution.py:275
  964.7 5.5 shard_map.80
  970.3 42.2 %all-to-all-done.9 = bf16[16,16,32,128]{3,2,1,0:T(8,128)(2,1)} async-done(((bf16[16,16,32,128]{3,2,1,0:T(8,128)(2,1)}), bf16[16,16,32,128]{3,2,1,0:T(8,128)(2,1)}, u32[]{:S(2)}, u32[]{:S(2)}) %all-to-all-start.9) | async-done | bytes 2097184 | tf_op jit(solution)/shard_map/all_to_all | solution.py:275
  1017.9 27.0 %shard_map.109 = (bf16[32,256,128]{2,1,0:T(8,128)(2,1)S(1)}, bf16[256,32,128]{2,1,0:T(8,128)(2,1)S(1)}) custom-call(s32[1]{0:T(128)S(6)} %convert_element_type.389.active, bf16[256,32,128]{2,1,0:T(8,128)(2,1)} %bitcast.44.back, bf16[32,256,128]{2,1,0:T(8,128)(2,1)} %copy-done.54, bf16[129,128,128]{2,1,0:T(8,128)(2,1)} %fusion.2.radial, ...), custom_call_target="tpu_custom_call" | custom-call | flops 4294967296 | bytes 8388608 | tf_op jit(solution)/shard_map/pallas_call | solution.py:230
  1047.6 17.3 all-to-all-done.3
  1071.4 27.0 %shard_map.102 = (bf16[32,256,128]{2,1,0:T(8,128)(2,1)S(1)}, bf16[256,32,128]{2,1,0:T(8,128)(2,1)S(1)}) custom-call(s32[1]{0:T(128)S(6)} %convert_element_type.384.active, bf16[256,32,128]{2,1,0:T(8,128)(2,1)} %bitcast.33.back, bf16[32,256,128]{2,1,0:T(8,128)(2,1)} %copy-done.53, bf16[129,128,128]{2,1,0:T(8,128)(2,1)} %fusion.2.radial, ...), custom_call_target="tpu_custom_call" | custom-call | flops 4294967296 | bytes 8388608 | tf_op jit(solution)/shard_map/pallas_call | solution.py:230
  1101.1 17.3 all-to-all-done.28.arrived
  1119.8 4.9 all-to-all-start.22
  1125.3 27.0 %shard_map.95 = (bf16[32,256,128]{2,1,0:T(8,128)(2,1)S(1)}, bf16[256,32,128]{2,1,0:T(8,128)(2,1)S(1)}) custom-call(s32[1]{0:T(128)S(6)} %convert_element_type.379.active, bf16[256,32,128]{2,1,0:T(8,128)(2,1)} %bitcast.24.back, bf16[32,256,128]{2,1,0:T(8,128)(2,1)} %copy-done.52, bf16[129,128,128]{2,1,0:T(8,128)(2,1)} %fusion.2.radial, ...), custom_call_target="tpu_custom_call" | custom-call | flops 4294967296 | bytes 8388608 | tf_op jit(solution)/shard_map/pallas_call | solution.py:230
  1155.0 17.2 all-to-all-done.22.arrived
  1172.3 4.7 all-to-all-start.16
  1177.6 27.0 %shard_map.88 = (bf16[32,256,128]{2,1,0:T(8,128)(2,1)S(1)}, bf16[256,32,128]{2,1,0:T(8,128)(2,1)S(1)}) custom-call(s32[1]{0:T(128)S(6)} %convert_element_type.374.active, bf16[256,32,128]{2,1,0:T(8,128)(2,1)} %bitcast.15.back, bf16[32,256,128]{2,1,0:T(8,128)(2,1)} %copy-done.50, bf16[129,128,128]{2,1,0:T(8,128)(2,1)} %fusion.2.radial, ...), custom_call_target="tpu_custom_call" | custom-call | flops 4294967296 | bytes 8388608 | tf_op jit(solution)/shard_map/pallas_call | solution.py:230
  1207.3 17.4 all-to-all-done.16.arrived
  1230.0 27.0 %shard_map.81 = (bf16[32,256,128]{2,1,0:T(8,128)(2,1)S(1)}, bf16[256,32,128]{2,1,0:T(8,128)(2,1)S(1)}) custom-call(s32[1]{0:T(128)S(6)} %convert_element_type.359.active, bf16[256,32,128]{2,1,0:T(8,128)(2,1)} %bitcast.108, bf16[32,256,128]{2,1,0:T(8,128)(2,1)} %copy-done.51, bf16[129,128,128]{2,1,0:T(8,128)(2,1)} %fusion.2.radial, ...), custom_call_target="tpu_custom_call" | custom-call | flops 4294967296 | bytes 8388608 | tf_op jit(solution)/shard_map/pallas_call | solution.py:230
  1259.7 17.4 all-to-all-done.10.arrived
  1289.2 40.4 %all-to-all-done.4.arrived = bf16[16,16,32,128]{3,2,1,0:T(8,128)(2,1)} async-done(((bf16[16,16,32,128]{3,2,1,0:T(8,128)(2,1)}), bf16[16,16,32,128]{3,2,1,0:T(8,128)(2,1)}, u32[]{:S(2)}, u32[]{:S(2)}) %all-to-all-start.4) | async-done | bytes 2097184 | tf_op jit(solution)/shard_map/all_to_all | solution.py:271
  1341.2 40.8 %all-to-all-done.29 = bf16[16,16,32,128]{3,2,1,0:T(8,128)(2,1)} async-done(((bf16[16,16,32,128]{3,2,1,0:T(8,128)(2,1)}), bf16[16,16,32,128]{3,2,1,0:T(8,128)(2,1)}, u32[]{:S(2)}, u32[]{:S(2)}) %all-to-all-start.29) | async-done | bytes 2097184 | tf_op jit(solution)/shard_map/all_to_all | solution.py:275
  1393.7 40.8 %all-to-all-done.17 = bf16[16,16,32,128]{3,2,1,0:T(8,128)(2,1)} async-done(((bf16[16,16,32,128]{3,2,1,0:T(8,128)(2,1)}), bf16[16,16,32,128]{3,2,1,0:T(8,128)(2,1)}, u32[]{:S(2)}, u32[]{:S(2)}) %all-to-all-start.17) | async-done | bytes 2097184 | tf_op jit(solution)/shard_map/all_to_all | solution.py:275
  1434.4 4.7 all-to-all-start.11
  1446.1 40.8 %all-to-all-done.11 = bf16[16,16,32,128]{3,2,1,0:T(8,128)(2,1)} async-done(((bf16[16,16,32,128]{3,2,1,0:T(8,128)(2,1)}), bf16[16,16,32,128]{3,2,1,0:T(8,128)(2,1)}, u32[]{:S(2)}, u32[]{:S(2)}) %all-to-all-start.11) | async-done | bytes 2097184 | tf_op jit(solution)/shard_map/all_to_all | solution.py:275
  1497.4 41.9 %all-to-all-done.5 = bf16[16,16,32,128]{3,2,1,0:T(8,128)(2,1)} async-done(((bf16[16,16,32,128]{3,2,1,0:T(8,128)(2,1)}), bf16[16,16,32,128]{3,2,1,0:T(8,128)(2,1)}, u32[]{:S(2)}, u32[]{:S(2)}) %all-to-all-start.5) | async-done | bytes 2097184 | tf_op jit(solution)/shard_map/all_to_all | solution.py:275
  1547.9 62.2 %psum.7 = f32[1]{0:T(128)} all-reduce(f32[1]{0:T(128)} %bitcast.51), channel_id=1, replica_groups=mesh['groups'=2,'pencil'=16] {'pencil'}, use_global_device_ids=true, to_apply=%region_1.2 | all-reduce | flops 1 | bytes 8 | tf_op jit(solution)/shard_map/psum | solution.py:347
  1614.1 24.2 %shard_map.111 = bf16[32,256,128]{2,1,0:T(8,128)(2,1)S(1)} custom-call(s32[1]{0:T(128)S(6)} %convert_element_type.388.active, bf16[256,32,128]{2,1,0:T(8,128)(2,1)} %bitcast.46.back, bf16[32,256,128]{2,1,0:T(8,128)(2,1)} %copy-done.46, bf16[129,128,128]{2,1,0:T(8,128)(2,1)} %fusion.2.radial, f32[32,128]{1,0:T(8,128)S(1)} %broadcast_in_dim.194.waves_squared, ...), custom_call_target="tpu_custom_call" | custom-call | flops 4294967296 | bytes 8388608 | tf_op jit(solution)/shard_map/pallas_call | solution.py:230
  1642.7 24.2 %shard_map.97 = bf16[32,256,128]{2,1,0:T(8,128)(2,1)S(1)} custom-call(s32[1]{0:T(128)S(6)} %convert_element_type.378.active, bf16[256,32,128]{2,1,0:T(8,128)(2,1)} %bitcast.26.back, bf16[32,256,128]{2,1,0:T(8,128)(2,1)} %copy-done.47, bf16[129,128,128]{2,1,0:T(8,128)(2,1)} %fusion.2.radial, f32[32,128]{1,0:T(8,128)S(1)} %broadcast_in_dim.194.waves_squared, ...), custom_call_target="tpu_custom_call" | custom-call | flops 4294967296 | bytes 8388608 | tf_op jit(solution)/shard_map/pallas_call | solution.py:230
  1667.0 24.2 %shard_map.90 = bf16[32,256,128]{2,1,0:T(8,128)(2,1)S(1)} custom-call(s32[1]{0:T(128)S(6)} %convert_element_type.373.active, bf16[256,32,128]{2,1,0:T(8,128)(2,1)} %bitcast.17.back, bf16[32,256,128]{2,1,0:T(8,128)(2,1)} %copy-done.48, bf16[129,128,128]{2,1,0:T(8,128)(2,1)} %fusion.2.radial, f32[32,128]{1,0:T(8,128)S(1)} %broadcast_in_dim.194.waves_squared, ...), custom_call_target="tpu_custom_call" | custom-call | flops 4294967296 | bytes 8388608 | tf_op jit(solution)/shard_map/pallas_call | solution.py:230
  1691.2 24.2 %shard_map.83 = bf16[32,256,128]{2,1,0:T(8,128)(2,1)S(1)} custom-call(s32[1]{0:T(128)S(6)} %convert_element_type.358.active, bf16[256,32,128]{2,1,0:T(8,128)(2,1)} %bitcast.8.back, bf16[32,256,128]{2,1,0:T(8,128)(2,1)} %copy-done.49, bf16[129,128,128]{2,1,0:T(8,128)(2,1)} %fusion.2.radial, f32[32,128]{1,0:T(8,128)S(1)} %broadcast_in_dim.194.waves_squared, ...), custom_call_target="tpu_custom_call" | custom-call | flops 4294967296 | bytes 8388608 | tf_op jit(solution)/shard_map/pallas_call | solution.py:230
  1728.4 23.9 %shard_map.104 = bf16[32,256,128]{2,1,0:T(8,128)(2,1)S(1)} custom-call(s32[1]{0:T(128)S(6)} %convert_element_type.383.active, bf16[256,32,128]{2,1,0:T(8,128)(2,1)S(1)} %bitcast.96, bf16[32,256,128]{2,1,0:T(8,128)(2,1)} %copy-done.45, bf16[129,128,128]{2,1,0:T(8,128)(2,1)} %fusion.2.radial, f32[32,128]{1,0:T(8,128)S(1)} %broadcast_in_dim.194.waves_squared, ...), custom_call_target="tpu_custom_call" | custom-call | flops 4294967296 | bytes 8388608 | tf_op jit(solution)/shard_map/pallas_call | solution.py:230
  1756.8 9.4 fusion.4
  (175 shorter events, 249.9 us)
Async XLA Ops:
  7.7 5.2 copy-start.4
  7.7 170.0 %copy-start = (bf16[32,256,128]{2,1,0:T(8,128)(2,1)}, bf16[32,256,128]{2,1,0:T(8,128)(2,1)S(1)}, u32[]{:S(2)}) copy-start(bf16[32,256,128]{2,1,0:T(8,128)(2,1)S(1)} %get-tuple-element.45.state) | copy-start | bytes 6291460
  12.9 1.3 copy-start.9
  14.2 53.9 %all-to-all-start.24 = ((bf16[16,16,32,128]{3,2,1,0:T(8,128)(2,1)}), bf16[16,16,32,128]{3,2,1,0:T(8,128)(2,1)}, u32[]{:S(2)}, u32[]{:S(2)}) async-start(bf16[16,16,32,128]{3,2,1,0:T(8,128)(2,1)} %bitcast.95), calls=%async_computation.24 | async-start | bytes 4194304 | tf_op jit(solution)/shard_map/all_to_all | solution.py:271
  20.4 1.6 copy-start.3
  68.2 52.4 %all-to-all-start.18 = ((bf16[16,16,32,128]{3,2,1,0:T(8,128)(2,1)}), bf16[16,16,32,128]{3,2,1,0:T(8,128)(2,1)}, u32[]{:S(2)}, u32[]{:S(2)}) async-start(bf16[16,16,32,128]{3,2,1,0:T(8,128)(2,1)} %bitcast.93), calls=%async_computation.18 | async-start | bytes 4194304 | tf_op jit(solution)/shard_map/all_to_all | solution.py:271
  72.9 1.6 copy-start.2
  120.6 52.4 %all-to-all-start.12 = ((bf16[16,16,32,128]{3,2,1,0:T(8,128)(2,1)}), bf16[16,16,32,128]{3,2,1,0:T(8,128)(2,1)}, u32[]{:S(2)}, u32[]{:S(2)}) async-start(bf16[16,16,32,128]{3,2,1,0:T(8,128)(2,1)} %bitcast.94), calls=%async_computation.12 | async-start | bytes 4194304 | tf_op jit(solution)/shard_map/all_to_all | solution.py:271
  125.3 1.6 copy-start.1
  173.0 52.4 %all-to-all-start.6 = ((bf16[16,16,32,128]{3,2,1,0:T(8,128)(2,1)}), bf16[16,16,32,128]{3,2,1,0:T(8,128)(2,1)}, u32[]{:S(2)}, u32[]{:S(2)}) async-start(bf16[16,16,32,128]{3,2,1,0:T(8,128)(2,1)} %bitcast.92), calls=%async_computation.6 | async-start | bytes 4194304 | tf_op jit(solution)/shard_map/all_to_all | solution.py:271
  180.5 1.3 copy-start.5
  225.5 4.8 copy-start.58
  225.5 52.5 %all-to-all-start = ((bf16[16,16,32,128]{3,2,1,0:T(8,128)(2,1)}), bf16[16,16,32,128]{3,2,1,0:T(8,128)(2,1)S(1)}, u32[]{:S(2)}, u32[]{:S(2)}) async-start(bf16[16,16,32,128]{3,2,1,0:T(8,128)(2,1)} %bitcast.91), calls=%async_computation | async-start | bytes 4194304 | tf_op jit(solution)/shard_map/all_to_all | solution.py:271
  277.9 52.4 %all-to-all-start.25 = ((bf16[16,16,32,128]{3,2,1,0:T(8,128)(2,1)}), bf16[16,16,32,128]{3,2,1,0:T(8,128)(2,1)}, u32[]{:S(2)}, u32[]{:S(2)}) async-start(bf16[16,16,32,128]{3,2,1,0:T(8,128)(2,1)} %copy-done.29), calls=%async_computation.25 | async-start | bytes 4194304 | tf_op jit(solution)/shard_map/all_to_all | solution.py:275
  288.3 1.3 copy-start.30
  330.4 52.4 %all-to-all-start.19 = ((bf16[16,16,32,128]{3,2,1,0:T(8,128)(2,1)}), bf16[16,16,32,128]{3,2,1,0:T(8,128)(2,1)}, u32[]{:S(2)}, u32[]{:S(2)}) async-start(bf16[16,16,32,128]{3,2,1,0:T(8,128)(2,1)} %copy-done.30), calls=%async_computation.19 | async-start | bytes 4194304 | tf_op jit(solution)/shard_map/all_to_all | solution.py:275
  340.7 1.3 copy-start.31
  382.8 52.6 %all-to-all-start.13 = ((bf16[16,16,32,128]{3,2,1,0:T(8,128)(2,1)}), bf16[16,16,32,128]{3,2,1,0:T(8,128)(2,1)}, u32[]{:S(2)}, u32[]{:S(2)}) async-start(bf16[16,16,32,128]{3,2,1,0:T(8,128)(2,1)} %copy-done.31), calls=%async_computation.13 | async-start | bytes 4194304 | tf_op jit(solution)/shard_map/all_to_all | solution.py:275
  393.5 1.3 copy-start.28
  435.4 52.4 %all-to-all-start.7 = ((bf16[16,16,32,128]{3,2,1,0:T(8,128)(2,1)}), bf16[16,16,32,128]{3,2,1,0:T(8,128)(2,1)}, u32[]{:S(2)}, u32[]{:S(2)}) async-start(bf16[16,16,32,128]{3,2,1,0:T(8,128)(2,1)} %copy-done.28), calls=%async_computation.7 | async-start | bytes 4194304 | tf_op jit(solution)/shard_map/all_to_all | solution.py:275
  445.9 46.6 %copy-start.56 = (bf16[129,64,64]{0,2,1:T(8,128)(2,1)S(1)}, bf16[129,64,64]{0,2,1:T(8,128)(2,1)}, u32[]{:S(2)}) copy-start(bf16[129,64,64]{0,2,1:T(8,128)(2,1)} %param.8) | copy-start | bytes 3170308
  487.9 52.4 %all-to-all-start.1 = ((bf16[16,16,32,128]{3,2,1,0:T(8,128)(2,1)}), bf16[16,16,32,128]{3,2,1,0:T(8,128)(2,1)}, u32[]{:S(2)}, u32[]{:S(2)}) async-start(bf16[16,16,32,128]{3,2,1,0:T(8,128)(2,1)} %copy-done.13), calls=%async_computation.1 | async-start | bytes 4194304 | tf_op jit(solution)/shard_map/all_to_all | solution.py:275
  492.6 4.3 copy-start.59
  530.2 1.3 copy-start.19
  531.6 1.3 copy-start.54
  540.3 52.3 %all-to-all-start.26 = ((bf16[16,16,32,128]{3,2,1,0:T(8,128)(2,1)}), bf16[16,16,32,128]{3,2,1,0:T(8,128)(2,1)S(1)}, u32[]{:S(2)}, u32[]{:S(2)}) async-start(bf16[16,16,32,128]{3,2,1,0:T(8,128)(2,1)} %bitcast.102), calls=%async_computation.26 | async-start | bytes 4194304 | tf_op jit(solution)/shard_map/all_to_all | solution.py:271
  572.6 1.3 copy-start.20
  592.6 52.4 %all-to-all-start.20 = ((bf16[16,16,32,128]{3,2,1,0:T(8,128)(2,1)}), bf16[16,16,32,128]{3,2,1,0:T(8,128)(2,1)}, u32[]{:S(2)}, u32[]{:S(2)}) async-start(bf16[16,16,32,128]{3,2,1,0:T(8,128)(2,1)} %bitcast.103), calls=%async_computation.20 | async-start | bytes 4194304 | tf_op jit(solution)/shard_map/all_to_all | solution.py:271
  624.9 1.3 copy-start.21
  645.1 52.4 %all-to-all-start.14 = ((bf16[16,16,32,128]{3,2,1,0:T(8,128)(2,1)}), bf16[16,16,32,128]{3,2,1,0:T(8,128)(2,1)}, u32[]{:S(2)}, u32[]{:S(2)}) async-start(bf16[16,16,32,128]{3,2,1,0:T(8,128)(2,1)} %bitcast.104), calls=%async_computation.14 | async-start | bytes 4194304 | tf_op jit(solution)/shard_map/all_to_all | solution.py:271
  677.5 1.3 copy-start.14
  678.8 1.3 copy-start.50
  697.5 52.8 %all-to-all-start.8 = ((bf16[16,16,32,128]{3,2,1,0:T(8,128)(2,1)}), bf16[16,16,32,128]{3,2,1,0:T(8,128)(2,1)}, u32[]{:S(2)}, u32[]{:S(2)}) async-start(bf16[16,16,32,128]{3,2,1,0:T(8,128)(2,1)} %bitcast.97), calls=%async_computation.8 | async-start | bytes 4194304 | tf_op jit(solution)/shard_map/all_to_all | solution.py:271
  730.4 1.3 copy-start.23
  731.7 1.4 copy-start.51
  750.3 52.4 %all-to-all-start.2 = ((bf16[16,16,32,128]{3,2,1,0:T(8,128)(2,1)}), bf16[16,16,32,128]{3,2,1,0:T(8,128)(2,1)}, u32[]{:S(2)}, u32[]{:S(2)}) async-start(bf16[16,16,32,128]{3,2,1,0:T(8,128)(2,1)} %bitcast.106), calls=%async_computation.2 | async-start | bytes 4194304 | tf_op jit(solution)/shard_map/all_to_all | solution.py:271
  759.5 1.3 copy-start.32
  760.8 46.6 %copy-start.39 = (bf16[512,512]{1,0:T(8,128)(2,1)S(1)}, bf16[512,512]{1,0:T(8,128)(2,1)}, u32[]{:S(2)}) copy-start(bf16[512,512]{1,0:T(8,128)(2,1)} %copy-done.33) | copy-start | bytes 1572868
  802.8 52.4 %all-to-all-start.27 = ((bf16[16,16,32,128]{3,2,1,0:T(8,128)(2,1)}), bf16[16,16,32,128]{3,2,1,0:T(8,128)(2,1)}, u32[]{:S(2)}, u32[]{:S(2)}) async-start(bf16[16,16,32,128]{3,2,1,0:T(8,128)(2,1)} %copy-done.32), calls=%async_computation.27 | async-start | bytes 4194304 | tf_op jit(solution)/shard_map/all_to_all | solution.py:275
  855.2 52.4 %all-to-all-start.21 = ((bf16[16,16,32,128]{3,2,1,0:T(8,128)(2,1)}), bf16[16,16,32,128]{3,2,1,0:T(8,128)(2,1)}, u32[]{:S(2)}, u32[]{:S(2)}) async-start(bf16[16,16,32,128]{3,2,1,0:T(8,128)(2,1)} %shard_map.101), calls=%async_computation.21 | async-start | bytes 4194304 | tf_op jit(solution)/shard_map/all_to_all | solution.py:275
  907.6 52.4 %all-to-all-start.15 = ((bf16[16,16,32,128]{3,2,1,0:T(8,128)(2,1)}), bf16[16,16,32,128]{3,2,1,0:T(8,128)(2,1)}, u32[]{:S(2)}, u32[]{:S(2)}) async-start(bf16[16,16,32,128]{3,2,1,0:T(8,128)(2,1)} %shard_map.94), calls=%async_computation.15 | async-start | bytes 4194304 | tf_op jit(solution)/shard_map/all_to_all | solution.py:275
  960.1 52.4 %all-to-all-start.9 = ((bf16[16,16,32,128]{3,2,1,0:T(8,128)(2,1)}), bf16[16,16,32,128]{3,2,1,0:T(8,128)(2,1)}, u32[]{:S(2)}, u32[]{:S(2)}) async-start(bf16[16,16,32,128]{3,2,1,0:T(8,128)(2,1)} %shard_map.87), calls=%async_computation.9 | async-start | bytes 4194304 | tf_op jit(solution)/shard_map/all_to_all | solution.py:275
  1012.5 52.3 %all-to-all-start.3 = ((bf16[16,16,32,128]{3,2,1,0:T(8,128)(2,1)}), bf16[16,16,32,128]{3,2,1,0:T(8,128)(2,1)S(1)}, u32[]{:S(2)}, u32[]{:S(2)}) async-start(bf16[16,16,32,128]{3,2,1,0:T(8,128)(2,1)} %shard_map.80), calls=%async_computation.3 | async-start | bytes 4194304 | tf_op jit(solution)/shard_map/all_to_all | solution.py:275
  1044.9 1.3 copy-start.16
  1046.2 1.3 copy-start.46
  1066.1 52.3 %all-to-all-start.28 = ((bf16[16,16,32,128]{3,2,1,0:T(8,128)(2,1)}), bf16[16,16,32,128]{3,2,1,0:T(8,128)(2,1)S(1)}, u32[]{:S(2)}, u32[]{:S(2)}) async-start(bf16[16,16,32,128]{3,2,1,0:T(8,128)(2,1)} %bitcast.99), calls=%async_computation.28 | async-start | bytes 4194304 | tf_op jit(solution)/shard_map/all_to_all | solution.py:271
  1098.5 1.4 copy-start.17
  1119.8 52.5 %all-to-all-start.22 = ((bf16[16,16,32,128]{3,2,1,0:T(8,128)(2,1)}), bf16[16,16,32,128]{3,2,1,0:T(8,128)(2,1)S(1)}, u32[]{:S(2)}, u32[]{:S(2)}) async-start(bf16[16,16,32,128]{3,2,1,0:T(8,128)(2,1)} %bitcast.100), calls=%async_computation.22 | async-start | bytes 4194304 | tf_op jit(solution)/shard_map/all_to_all | solution.py:271
  1152.4 1.3 copy-start.18
  1172.3 52.4 %all-to-all-start.16 = ((bf16[16,16,32,128]{3,2,1,0:T(8,128)(2,1)}), bf16[16,16,32,128]{3,2,1,0:T(8,128)(2,1)}, u32[]{:S(2)}, u32[]{:S(2)}) async-start(bf16[16,16,32,128]{3,2,1,0:T(8,128)(2,1)} %bitcast.101), calls=%async_computation.16 | async-start | bytes 4194304 | tf_op jit(solution)/shard_map/all_to_all | solution.py:271
  1204.7 1.4 copy-start.15
  1206.0 1.3 copy-start.48
  1224.7 52.4 %all-to-all-start.10 = ((bf16[16,16,32,128]{3,2,1,0:T(8,128)(2,1)}), bf16[16,16,32,128]{3,2,1,0:T(8,128)(2,1)}, u32[]{:S(2)}, u32[]{:S(2)}) async-start(bf16[16,16,32,128]{3,2,1,0:T(8,128)(2,1)} %bitcast.98), calls=%async_computation.10 | async-start | bytes 4194304 | tf_op jit(solution)/shard_map/all_to_all | solution.py:271
  1258.4 1.3 copy-start.49
  1277.1 52.4 %all-to-all-start.4 = ((bf16[16,16,32,128]{3,2,1,0:T(8,128)(2,1)}), bf16[16,16,32,128]{3,2,1,0:T(8,128)(2,1)}, u32[]{:S(2)}, u32[]{:S(2)}) async-start(bf16[16,16,32,128]{3,2,1,0:T(8,128)(2,1)} %bitcast.105), calls=%async_computation.4 | async-start | bytes 4194304 | tf_op jit(solution)/shard_map/all_to_all | solution.py:271
  1281.8 1.6 copy-start.12
  1329.6 52.4 %all-to-all-start.29 = ((bf16[16,16,32,128]{3,2,1,0:T(8,128)(2,1)}), bf16[16,16,32,128]{3,2,1,0:T(8,128)(2,1)}, u32[]{:S(2)}, u32[]{:S(2)}) async-start(bf16[16,16,32,128]{3,2,1,0:T(8,128)(2,1)} %copy-done.25), calls=%async_computation.29 | async-start | bytes 4194304 | tf_op jit(solution)/shard_map/all_to_all | solution.py:275
  1382.0 52.4 %all-to-all-start.17 = ((bf16[16,16,32,128]{3,2,1,0:T(8,128)(2,1)}), bf16[16,16,32,128]{3,2,1,0:T(8,128)(2,1)}, u32[]{:S(2)}, u32[]{:S(2)}) async-start(bf16[16,16,32,128]{3,2,1,0:T(8,128)(2,1)} %copy-done.26), calls=%async_computation.17 | async-start | bytes 4194304 | tf_op jit(solution)/shard_map/all_to_all | solution.py:275
  1392.3 1.3 copy-start.27
  1434.4 52.4 %all-to-all-start.11 = ((bf16[16,16,32,128]{3,2,1,0:T(8,128)(2,1)}), bf16[16,16,32,128]{3,2,1,0:T(8,128)(2,1)}, u32[]{:S(2)}, u32[]{:S(2)}) async-start(bf16[16,16,32,128]{3,2,1,0:T(8,128)(2,1)} %copy-done.27), calls=%async_computation.11 | async-start | bytes 4194304 | tf_op jit(solution)/shard_map/all_to_all | solution.py:275
  1486.9 52.4 %all-to-all-start.5 = ((bf16[16,16,32,128]{3,2,1,0:T(8,128)(2,1)}), bf16[16,16,32,128]{3,2,1,0:T(8,128)(2,1)}, u32[]{:S(2)}, u32[]{:S(2)}) async-start(bf16[16,16,32,128]{3,2,1,0:T(8,128)(2,1)} %copy-done.24), calls=%async_computation.5 | async-start | bytes 4194304 | tf_op jit(solution)/shard_map/all_to_all | solution.py:275
  1496.0 1.4 copy-start.10
  1539.3 189.1 %all-to-all-start.23 = ((bf16[16,16,32,128]{3,2,1,0:T(8,128)(2,1)}), bf16[16,16,32,128]{3,2,1,0:T(8,128)(2,1)S(1)}, u32[]{:S(2)}, u32[]{:S(2)}) async-start(bf16[16,16,32,128]{3,2,1,0:T(8,128)(2,1)} %copy-done.10), calls=%async_computation.23 | async-start | bytes 4194304 | tf_op jit(solution)/shard_map/all_to_all | solution.py:275
  1752.3 4.5 copy-start.55
  (26 other events, 30.9 us)

commit v2 on v1

--- a/solution.py
+++ b/solution.py
@@ -79,7 +79,11 @@
 
 
 def swap_block(source, first, second):
-    block = source[pl.ds(first, BLOCK), pl.ds(second, BLOCK), :].astype(jnp.float32)
+    if len(source.shape) == 4:
+        block = source[first // BLOCK, :, pl.ds(second, BLOCK), :]
+    else:
+        block = source[pl.ds(first, BLOCK), pl.ds(second, BLOCK), :]
+    block = block.astype(jnp.float32)
     return jnp.swapaxes(block, 0, 1).astype(jnp.bfloat16)
 
 
@@ -87,7 +91,11 @@
     def one(index, _):
         first = pl.multiple_of(index * BLOCK, BLOCK)
         for second in range(0, columns, BLOCK):
-            target[pl.ds(second, BLOCK), pl.ds(first, BLOCK), :] = swap_block(source, first, second)
+            block = swap_block(source, first, second)
+            if len(target.shape) == 4:
+                target[second // BLOCK, :, pl.ds(first, BLOCK), :] = block
+            else:
+                target[pl.ds(second, BLOCK), pl.ds(first, BLOCK), :] = block
         return 0
 
     lax.fori_loop(0, rows // BLOCK, one, 0)
@@ -112,20 +120,35 @@
     analyse(state, table, spread, out, local_z, azimuths)
 
 
-def start_call(state, table_azimuth):
-    local_z, azimuths, channels = state.shape
-    vmem = pl.BlockSpec(memory_space=pltpu.VMEM)
+def field_block(fields, offset):
+    shape = (None,) + fields.shape[1:]
+    return pl.BlockSpec(shape, lambda s: (s + offset, 0, 0, 0))
+
+
+def sent_block(shape):
+    pencils, _, points, local_z, channels = shape
+    return pl.BlockSpec((pencils, None, points, local_z, channels), lambda s: (0, s, 0, 0, 0))
+
+
+def whole_block(array):
+    return pl.BlockSpec(array.shape, lambda s: (0,) * array.ndim)
+
+
+def start_call(states, offset, table_azimuth, shape):
+    _, local_z, azimuths, channels = states.shape
+    size = shape[1] * local_z * azimuths * channels
     return pl.pallas_call(
         start_kernel,
-        out_shape=jax.ShapeDtypeStruct((azimuths, local_z, channels), jnp.bfloat16),
-        in_specs=[vmem, vmem],
-        out_specs=vmem,
-        scratch_shapes=[pltpu.VMEM(state.shape, jnp.bfloat16)],
+        grid=(shape[1],),
+        out_shape=jax.ShapeDtypeStruct(shape, jnp.bfloat16),
+        in_specs=[field_block(states, offset), whole_block(table_azimuth)],
+        out_specs=sent_block(shape),
+        scratch_shapes=[pltpu.VMEM((local_z, azimuths, channels), jnp.bfloat16)],
         compiler_params=pltpu.CompilerParams(vmem_limit_bytes=VMEM_BYTES),
         cost_estimate=pl.CostEstimate(
-            flops=2 * azimuths * state.size, bytes_accessed=6 * state.size, transcendentals=0
+            flops=2 * azimuths * size, bytes_accessed=6 * size, transcendentals=0
         ),
-    )(state, table_azimuth)
+    )(states, table_azimuth)
 
 
 def middle_kernel(arrived, base, table, table_t, out):
@@ -146,16 +169,19 @@
 
 
 def middle_call(arrived, base, table, table_t):
-    pencils, points, local_z, channels = arrived.shape
+    pencils, group, points, local_z, channels = arrived.shape
     total_z = pencils * local_z
     count = 4
-    block = pl.BlockSpec((pencils, count, local_z, channels), lambda p: (0, p, 0, 0))
-    whole = pl.BlockSpec((total_z, total_z), lambda p: (0, 0))
+    block = pl.BlockSpec(
+        (pencils, None, count, local_z, channels), lambda s, p: (0, s, p, 0, 0)
+    )
+    whole = pl.BlockSpec((total_z, total_z), lambda s, p: (0, 0))
+    base_block = pl.BlockSpec((None, count, 1, total_z), lambda s, p: (s, p, 0, 0))
     return pl.pallas_call(
         middle_kernel,
-        grid=(points // count,),
+        grid=(group, points // count),
         out_shape=jax.ShapeDtypeStruct(arrived.shape, jnp.bfloat16),
-        in_specs=[block, pl.BlockSpec((count, 1, total_z), lambda p: (p, 0, 0)), whole, whole],
+        in_specs=[block, base_block, whole, whole],
         out_specs=block,
         compiler_params=pltpu.CompilerParams(vmem_limit_bytes=VMEM_BYTES),
         cost_estimate=pl.CostEstimate(
@@ -210,7 +236,7 @@
     for wave in range(1 + loops * group, half):
         radial_step(wave, 2 * wave - 1, 2)
     swap_all(by_mode, spread, azimuths, local_z)
-    keep = active[0] > 0
+    keep = active[pl.program_id(0)] > 0
 
     def choose(index, _):
         new_state[index] = jnp.where(keep, spread[index], state[index])
@@ -221,73 +247,93 @@
         analyse(new_state, table, spread, out, local_z, azimuths)
 
 
-def finish_call(last, active, back, state, radial, waves_squared, table, table_t):
-    local_z, azimuths, channels = state.shape
-    vmem = pl.BlockSpec(memory_space=pltpu.VMEM)
-    state_shape = jax.ShapeDtypeStruct(state.shape, jnp.bfloat16)
-    out_shape = jax.ShapeDtypeStruct(back.shape, jnp.bfloat16)
-    shapes = [state_shape] if last else [state_shape, out_shape]
+def finish_call(last, active, back, states, offset, radial, waves_squared, table, table_t):
+    _, local_z, azimuths, channels = states.shape
+    group = back.shape[1]
+    fields = jax.ShapeDtypeStruct((group, local_z, azimuths, channels), jnp.bfloat16)
+    shapes = [fields] if last else [fields, jax.ShapeDtypeStruct(back.shape, jnp.bfloat16)]
+    blocks = [field_block(fields, 0)] + ([] if last else [sent_block(back.shape)])
     return pl.pallas_call(
         functools.partial(finish_kernel, last),
+        grid=(group,),
         out_shape=shapes,
-        in_specs=[pl.BlockSpec(memory_space=pltpu.SMEM)] + [vmem] * 6,
-        out_specs=[vmem] * len(shapes),
+        in_specs=[
+            pl.BlockSpec(memory_space=pltpu.SMEM),
+            sent_block(back.shape),
+            field_block(states, offset),
+            whole_block(radial),
+            whole_block(waves_squared),
+            whole_block(table),
+            whole_block(table_t),
+        ],
+        out_specs=blocks,
         scratch_shapes=[
-            pltpu.VMEM(state.shape, jnp.bfloat16),
-            pltpu.VMEM(back.shape, jnp.bfloat16),
+            pltpu.VMEM((local_z, azimuths, channels), jnp.bfloat16),
+            pltpu.VMEM((azimuths, local_z, channels), jnp.bfloat16),
         ],
         compiler_params=pltpu.CompilerParams(vmem_limit_bytes=VMEM_BYTES),
         cost_estimate=pl.CostEstimate(
-            flops=4 * azimuths * state.size * 4, bytes_accessed=8 * state.size, transcendentals=0
+            flops=16 * azimuths * fields.size, bytes_accessed=8 * fields.size, transcendentals=0
         ),
-    )(active, back, state, radial, waves_squared, table, table_t)
-
-
-def run_kernels(states, base_wave, radial_inverse, step_counts, waves_axial, tables):
-    segments = len(states)
-    local_z, azimuths, channels = states[0].shape
+    )(active, back, states, radial, waves_squared, table, table_t)
+
+
+def run_kernels(
+    krylov_vector, base_wave, radial_inverse, step_counts, waves_axial, tables, phase_value
+):
+    segments, local_z, azimuths, channels = krylov_vector.shape
     points = base_wave.shape[1]
     pencils = azimuths // points
     table_azimuth, table_axial = tables
     transposed = jnp.swapaxes(radial_inverse, 1, 2)
     blank = jnp.zeros_like(transposed)
-    radial = transposed
-    if channels != radial.shape[1]:
-        radial = jnp.concatenate(
-            [
-                jnp.concatenate([transposed, blank], axis=2),
-                jnp.concatenate([blank, transposed], axis=2),
-            ],
-            axis=1,
-        )
+    radial = jnp.concatenate(
+        [
+            jnp.concatenate([transposed, blank], axis=2),
+            jnp.concatenate([blank, transposed], axis=2),
+        ],
+        axis=1,
+    )
     waves_f = waves_axial.astype(jnp.float32)
     waves_squared = jnp.broadcast_to((waves_f * waves_f)[:, None], (local_z, channels))
     base = base_wave.astype(jnp.float32)[:, :, None, :]
-    shape = (pencils, points, local_z, channels)
-    sent = [start_call(states[s], table_azimuth) for s in range(segments)]
+    later_table, phase_value = lax.optimization_barrier((table_azimuth, phase_value))
+    first_size = (segments + 1) // 2
+    groups = [(0, first_size), (first_size, segments)]
+    states = [krylov_vector] * len(groups)
+    offsets = [begin for begin, _ in groups]
+    sent = [
+        start_call(
+            krylov_vector,
+            begin,
+            later_table if begin == 0 else table_azimuth,
+            (pencils, end - begin, points, local_z, channels),
+        )
+        for begin, end in groups
+    ]
     for step_index in range(NSTEP):
         last = step_index == NSTEP - 1
-        for s in range(segments):
-            arrived = lax.all_to_all(
-                sent[s].reshape(shape), "pencil", split_axis=0, concat_axis=0, tiled=True
-            )
-            product = middle_call(arrived, base[s], table_axial, table_axial.T)
+        for g, (begin, end) in enumerate(groups):
+            arrived = lax.all_to_all(sent[g], "pencil", split_axis=0, concat_axis=0, tiled=True)
+            product = middle_call(arrived, base[begin:end], table_axial, table_axial.T)
             back = lax.all_to_all(product, "pencil", split_axis=0, concat_axis=0, tiled=True)
-            active = (step_index < step_counts[s : s + 1]).astype(jnp.int32)
+            active = (step_index < step_counts[begin:end]).astype(jnp.int32)
             results = finish_call(
                 last,
                 active,
-                back.reshape(azimuths, local_z, channels),
-                states[s],
+                back,
+                states[g],
+                offsets[g],
                 radial,
                 waves_squared,
                 table_azimuth,
                 table_azimuth.T,
             )
-            states[s] = results[0]
+            states[g], offsets[g] = results[0], 0
             if not last:
-                sent[s] = results[1]
-    return states
+                sent[g] = results[1]
+    ends = [states[g][i] for g, (begin, end) in enumerate(groups) for i in range(end - begin)]
+    return ends, phase_value
 
 
 def body(krylov_vector, base_wave, radial_inverse, step_counts, azimuth_shift, phase_tangent):
@@ -299,21 +345,25 @@
     damping_factor = damping(axial_index, azimuths)
     radial_full = expand_radial(radial_inverse, azimuths)
     states = [krylov_vector[s] for s in range(segments)]
+    local_phase = jnp.sum(phase_tangent.astype(jnp.float32) * krylov_vector[0].astype(jnp.float32))
+    phase_value = lax.psum(local_phase, "pencil").reshape(1)
     fits = (
         local_z % BLOCK == 0
         and azimuths % BLOCK == 0
-        and base_wave.shape[1] % 4 == 0
+        and base_wave.shape[1] == BLOCK
+        and segments > 1
         and channels == 128
         and channels == 2 * radial_inverse.shape[1]
     )
     if fits:
-        states = run_kernels(
-            states,
+        states, phase_value = run_kernels(
+            krylov_vector,
             base_wave,
             radial_inverse,
             step_counts,
             (axial_index + 1) // 2,
             (table_azimuth, table_axial),
+            phase_value,
         )
     else:
         for step_index in range(NSTEP):
@@ -343,8 +393,6 @@
         + [shifted - krylov_vector[0].astype(jnp.float32)],
         axis=0,
     )
-    local_phase = jnp.sum(phase_tangent.astype(jnp.float32) * krylov_vector[0].astype(jnp.float32))
-    phase_value = lax.psum(local_phase, "pencil").reshape(1)
     return (shooting, phase_value)
 
 

time: 1780 us -> 1580 us (0.89)
  starting transfers between devices: 143 us -> 57.9 us
  waiting for transfers between devices: 945 us -> 879 us
  blocking collectives: 62.2 us -> 108 us
  local copies, waits for them, and re-layouts: 79.9 us -> 36.4 us
  Pallas kernels: 473 us -> 452 us
    psum x1, blocking collectives: 62.2 us -> 108 us  [body(): phase_value = lax.psum(local_phase, 'pencil').reshape(1)]
    all_to_all x15 -> x6, waiting for transfers between devices: 522 us -> 477 us  [run_kernels(): lax.all_to_all(product, 'pencil', split_axis=0, concat_axis=0, tiled=True)]
    all_to_all x15 -> x6, starting transfers between devices: 72.7 us -> 29.8 us  [run_kernels(): lax.all_to_all(sent[g], 'pencil', split_axis=0, concat_axis=0, tiled=True)]
    all_to_all x15 -> x6, starting transfers between devices: 70.6 us -> 28.1 us  [run_kernels(): lax.all_to_all(product, 'pencil', split_axis=0, concat_axis=0, tiled=True)]
    unnamed x121 -> x35, local copies, waits for them, and re-layouts: 72.1 us -> 36.2 us
    pallas_call x35 -> x14, Pallas kernels: 473 us -> 452 us  [the longest x6 367 us: finish_call(): pl.pallas_call(functools.partial(finish_kernel, last), grid=(group,), out...]
    all_to_all x15 -> x6, waiting for transfers between devices: 423 us -> 402 us  [run_kernels(): lax.all_to_all(sent[g], 'pencil', split_axis=0, concat_axis=0, tiled=True)]
  transfers between devices with their start and end apart: 30 -> 12, of which waited for: 29 -> 11; matrix products, arithmetic and copies ran while one was open for 2% -> 2% of each run, Pallas kernels for 25% -> 24%
where the time goes in v2:
time: 1580 us
  waiting for transfers between devices  879 us (56%)
  Pallas kernels  452 us (29%)
  blocking collectives  108 us (7%)
  starting transfers between devices  57.9 us (4%)
  local copies, waits for them, and re-layouts  36.4 us (2%)
  other arithmetic  30.2 us (2%)
    all_to_all x6, waiting for transfers between devices, run_kernels(): lax.all_to_all(product, 'pencil', split_axis=0, concat_axis=0, tiled=True)  477 us
    all_to_all x6, waiting for transfers between devices, run_kernels(): lax.all_to_all(sent[g], 'pencil', split_axis=0, concat_axis=0, tiled=True)  402 us
    pallas_call x6, Pallas kernels, finish_call(): pl.pallas_call(functools.partial(finish_kernel, last), grid=(group,), out...  367 us
    psum x1, blocking collectives, body(): phase_value = lax.psum(local_phase, 'pencil').reshape(1)  108 us
    pallas_call x6, Pallas kernels, middle_call(): pl.pallas_call(middle_kernel, grid=(group, points // count), out_shape=ja...  67 us
    unnamed x35, local copies, waits for them, and re-layouts  36.2 us
  transfers between devices with their start and end apart: 12, of which 11 were waited for; matrix products, arithmetic and copies ran while one was open for 2% of the time, Pallas kernels for 24%

profile of v2, /device:TPU:18, one launch (start us, length us, event | category | flops | bytes accessed | tf_op | source)
XLA Modules:
  0.0 1577.5 jit_solution(8003594996205542132)
XLA Ops:
  0.7 2.4 multiply_convert_fusion.2
  3.1 7.4 shard_map.84
  10.6 2.0 copy-done
  12.5 6.3 all-to-all-start.6
  18.9 3.3 fusion.3
  22.2 108.0 %psum.7 = f32[1]{0:T(128)} all-reduce(f32[1]{0:T(128)} %bitcast.1), channel_id=1, replica_groups=mesh['groups'=2,'pencil'=16] {'pencil'}, use_global_device_ids=true, to_apply=%region_1.2 | all-reduce | flops 1 | bytes 8 | tf_op jit(solution)/shard_map/psum | solution.py:349
  130.1 11.2 shard_map.77
  141.4 4.7 all-to-all-start
  146.2 9.1 multiply_convert_fusion
  155.3 8.4 shard_map.85
  163.7 2.0 copy-done.4
  165.8 117.6 %all-to-all-done.arrived = bf16[16,3,16,32,128]{4,3,2,1,0:T(8,128)(2,1)} async-done(((bf16[16,3,16,32,128]{4,3,2,1,0:T(8,128)(2,1)}), bf16[16,3,16,32,128]{4,3,2,1,0:T(8,128)(2,1)}, u32[]{:S(2)}, u32[]{:S(2)}) %all-to-all-start) | async-done | bytes 6291488 | tf_op jit(solution)/shard_map/all_to_all | solution.py:317
  283.4 4.7 all-to-all-start.7
  288.1 0.1 copy.8.base
  288.2 13.9 shard_map.78
  302.1 78.7 %all-to-all-done.7.back = bf16[16,2,16,32,128]{4,3,2,1,0:T(8,128)(2,1)} async-done(((bf16[16,2,16,32,128]{4,3,2,1,0:T(8,128)(2,1)}), bf16[16,2,16,32,128]{4,3,2,1,0:T(8,128)(2,1)}, u32[]{:S(2)}, u32[]{:S(2)}) %all-to-all-start.7) | async-done | bytes 4194336 | tf_op jit(solution)/shard_map/all_to_all | solution.py:319
  380.7 4.7 all-to-all-start.1
  385.5 6.3 copy.9
  391.8 4.9 fusion.2.radial
  396.8 52.1 %shard_map.86 = (bf16[2,32,256,128]{3,2,1,0:T(8,128)(2,1)S(1)}, bf16[16,2,16,32,128]{4,3,2,1,0:T(8,128)(2,1)}) custom-call(s32[2]{0:T(128)S(1)} %get-tuple-element.26.active, bf16[16,2,16,32,128]{4,3,2,1,0:T(8,128)(2,1)} %all-to-all-done.7.back, bf16[5,32,256,128]{3,2,1,0:T(8,128)(2,1)} %state.7, bf16[129,128,128]{2,1,0:T(8,128)(2,1)} %fusion.2.radial, ...), custom_call_target="tpu_custom_call" | custom-call | flops 8589934592 | bytes 16777216 | tf_op jit(solution)/shard_map/pallas_call | solution.py:256
  448.9 2.1 copy-done.9
  451.0 72.1 %all-to-all-done.1.back = bf16[16,3,16,32,128]{4,3,2,1,0:T(8,128)(2,1)} async-done(((bf16[16,3,16,32,128]{4,3,2,1,0:T(8,128)(2,1)}), bf16[16,3,16,32,128]{4,3,2,1,0:T(8,128)(2,1)}, u32[]{:S(2)}, u32[]{:S(2)}) %all-to-all-start.1) | async-done | bytes 6291488 | tf_op jit(solution)/shard_map/all_to_all | solution.py:319
  523.1 4.7 all-to-all-start.8
  527.8 2.2 copy-done.1
  530.0 75.3 %shard_map.79 = (bf16[3,32,256,128]{3,2,1,0:T(8,128)(2,1)}, bf16[16,3,16,32,128]{4,3,2,1,0:T(8,128)(2,1)}) custom-call(s32[3]{0:T(128)S(1)} %get-tuple-element.29.active, bf16[16,3,16,32,128]{4,3,2,1,0:T(8,128)(2,1)} %all-to-all-done.1.back, bf16[5,32,256,128]{3,2,1,0:T(8,128)(2,1)} %state.7, bf16[129,128,128]{2,1,0:T(8,128)(2,1)S(1)} %copy-done.1, ...), custom_call_target="tpu_custom_call" | custom-call | flops 12884901888 | bytes 25165824 | tf_op jit(solution)/shard_map/pallas_call | solution.py:256
  605.3 15.2 all-to-all-done.8.arrived
  620.4 4.7 all-to-all-start.2
  625.1 8.4 shard_map.87
  633.6 2.0 copy-done.6
  635.6 127.1 %all-to-all-done.2.arrived = bf16[16,3,16,32,128]{4,3,2,1,0:T(8,128)(2,1)} async-done(((bf16[16,3,16,32,128]{4,3,2,1,0:T(8,128)(2,1)}), bf16[16,3,16,32,128]{4,3,2,1,0:T(8,128)(2,1)}, u32[]{:S(2)}, u32[]{:S(2)}) %all-to-all-start.2) | async-done | bytes 6291488 | tf_op jit(solution)/shard_map/all_to_all | solution.py:317
  762.8 4.7 all-to-all-start.9
  767.4 13.9 shard_map.80
  781.3 78.8 %all-to-all-done.9.back = bf16[16,2,16,32,128]{4,3,2,1,0:T(8,128)(2,1)} async-done(((bf16[16,2,16,32,128]{4,3,2,1,0:T(8,128)(2,1)}), bf16[16,2,16,32,128]{4,3,2,1,0:T(8,128)(2,1)}, u32[]{:S(2)}, u32[]{:S(2)}) %all-to-all-start.9) | async-done | bytes 4194336 | tf_op jit(solution)/shard_map/all_to_all | solution.py:319
  860.1 4.7 all-to-all-start.3
  864.8 52.2 %shard_map.88 = (bf16[2,32,256,128]{3,2,1,0:T(8,128)(2,1)S(1)}, bf16[16,2,16,32,128]{4,3,2,1,0:T(8,128)(2,1)}) custom-call(s32[2]{0:T(128)S(1)} %get-tuple-element.27.active, bf16[16,2,16,32,128]{4,3,2,1,0:T(8,128)(2,1)} %all-to-all-done.9.back, bf16[2,32,256,128]{3,2,1,0:T(8,128)(2,1)} %copy-done.9, bf16[129,128,128]{2,1,0:T(8,128)(2,1)} %fusion.2.radial, ...), custom_call_target="tpu_custom_call" | custom-call | flops 8589934592 | bytes 16777216 | tf_op jit(solution)/shard_map/pallas_call | solution.py:256
  917.0 2.1 copy-done.10
  919.1 83.4 %all-to-all-done.3.back = bf16[16,3,16,32,128]{4,3,2,1,0:T(8,128)(2,1)} async-done(((bf16[16,3,16,32,128]{4,3,2,1,0:T(8,128)(2,1)}), bf16[16,3,16,32,128]{4,3,2,1,0:T(8,128)(2,1)}, u32[]{:S(2)}, u32[]{:S(2)}) %all-to-all-start.3) | async-done | bytes 6291488 | tf_op jit(solution)/shard_map/all_to_all | solution.py:319
  1002.4 4.7 all-to-all-start.10
  1007.1 2.2 copy-done.2
  1009.3 75.2 %shard_map.81 = (bf16[3,32,256,128]{3,2,1,0:T(8,128)(2,1)}, bf16[16,3,16,32,128]{4,3,2,1,0:T(8,128)(2,1)}) custom-call(s32[3]{0:T(128)S(1)} %get-tuple-element.30.active, bf16[16,3,16,32,128]{4,3,2,1,0:T(8,128)(2,1)} %all-to-all-done.3.back, bf16[3,32,256,128]{3,2,1,0:T(8,128)(2,1)} %get-tuple-element.14.state, bf16[129,128,128]{2,1,0:T(8,128)(2,1)S(1)} %copy-done.2, ...), custom_call_target="tpu_custom_call" | custom-call | flops 12884901888 | bytes 25165824 | tf_op jit(solution)/shard_map/pallas_call | solution.py:256
  1084.6 15.3 all-to-all-done.10.arrived
  1099.8 4.7 all-to-all-start.4
  1104.6 8.4 shard_map.89
  1113.0 2.0 copy-done.5
  1115.1 127.1 %all-to-all-done.4.arrived = bf16[16,3,16,32,128]{4,3,2,1,0:T(8,128)(2,1)} async-done(((bf16[16,3,16,32,128]{4,3,2,1,0:T(8,128)(2,1)}), bf16[16,3,16,32,128]{4,3,2,1,0:T(8,128)(2,1)}, u32[]{:S(2)}, u32[]{:S(2)}) %all-to-all-start.4) | async-done | bytes 6291488 | tf_op jit(solution)/shard_map/all_to_all | solution.py:317
  1242.1 4.7 all-to-all-start.11
  1246.8 13.9 shard_map.82
  1260.7 78.8 %all-to-all-done.11.back = bf16[16,2,16,32,128]{4,3,2,1,0:T(8,128)(2,1)} async-done(((bf16[16,2,16,32,128]{4,3,2,1,0:T(8,128)(2,1)}), bf16[16,2,16,32,128]{4,3,2,1,0:T(8,128)(2,1)}, u32[]{:S(2)}, u32[]{:S(2)}) %all-to-all-start.11) | async-done | bytes 4194336 | tf_op jit(solution)/shard_map/all_to_all | solution.py:319
  1339.5 4.7 all-to-all-start.5
  1344.9 45.4 %shard_map.90 = bf16[2,32,256,128]{3,2,1,0:T(8,128)(2,1)S(1)} custom-call(s32[2]{0:T(128)S(1)} %get-tuple-element.28.active, bf16[16,2,16,32,128]{4,3,2,1,0:T(8,128)(2,1)} %all-to-all-done.11.back, bf16[2,32,256,128]{3,2,1,0:T(8,128)(2,1)} %copy-done.10, bf16[129,128,128]{2,1,0:T(8,128)(2,1)} %fusion.2.radial, ...), custom_call_target="tpu_custom_call" | custom-call | flops 8589934592 | bytes 16777216 | tf_op jit(solution)/shard_map/pallas_call | solution.py:256
  1390.3 1.9 copy-done.7
  1392.2 4.4 convolution_bitcast_fusion
  1396.5 85.3 %all-to-all-done.5.back = bf16[16,3,16,32,128]{4,3,2,1,0:T(8,128)(2,1)} async-done(((bf16[16,3,16,32,128]{4,3,2,1,0:T(8,128)(2,1)}), bf16[16,3,16,32,128]{4,3,2,1,0:T(8,128)(2,1)}, u32[]{:S(2)}, u32[]{:S(2)}) %all-to-all-start.5) | async-done | bytes 6291488 | tf_op jit(solution)/shard_map/all_to_all | solution.py:319
  1481.8 2.2 copy-done.3
  1484.0 66.3 %shard_map.83 = bf16[3,32,256,128]{3,2,1,0:T(8,128)(2,1)} custom-call(s32[3]{0:T(128)S(1)} %get-tuple-element.31.active, bf16[16,3,16,32,128]{4,3,2,1,0:T(8,128)(2,1)} %all-to-all-done.5.back, bf16[3,32,256,128]{3,2,1,0:T(8,128)(2,1)} %get-tuple-element.16.state, bf16[129,128,128]{2,1,0:T(8,128)(2,1)S(1)} %copy-done.3, ...), custom_call_target="tpu_custom_call" | custom-call | flops 12884901888 | bytes 25165824 | tf_op jit(solution)/shard_map/pallas_call | solution.py:256
  1550.4 3.1 subtract_dynamic-update-slice_fusion.3
  1553.5 0.9 copy-done.11
  1554.4 2.3 subtract_dynamic-update-slice_fusion.2
  1556.7 2.4 subtract_dynamic-update-slice_fusion.1
  1559.1 0.4 copy-done.8
  1559.5 2.4 subtract_dynamic-update-slice_fusion
  1562.0 0.4 copy-done.12
  1562.3 7.6 fusion.5
  1570.0 7.5 copy-done.14
  (35 shorter events, 0.3 us)
Async XLA Ops:
  10.6 2.0 copy-start
  12.5 6.3 copy-start.13
  12.5 128.8 %all-to-all-start.6 = ((bf16[16,2,16,32,128]{4,3,2,1,0:T(8,128)(2,1)}), bf16[16,2,16,32,128]{4,3,2,1,0:T(8,128)(2,1)}, u32[]{:S(2)}, u32[]{:S(2)}) async-start(bf16[16,2,16,32,128]{4,3,2,1,0:T(8,128)(2,1)} %copy-done), calls=%async_computation.6 | async-start | bytes 8388608 | tf_op jit(solution)/shard_map/all_to_all | solution.py:317
  141.4 4.7 copy-start.15
  141.4 142.0 %all-to-all-start = ((bf16[16,3,16,32,128]{4,3,2,1,0:T(8,128)(2,1)}), bf16[16,3,16,32,128]{4,3,2,1,0:T(8,128)(2,1)}, u32[]{:S(2)}, u32[]{:S(2)}) async-start(bf16[16,3,16,32,128]{4,3,2,1,0:T(8,128)(2,1)} %shard_map.77), calls=%async_computation | async-start | bytes 12582912 | tf_op jit(solution)/shard_map/all_to_all | solution.py:317
  163.7 2.1 copy-start.4
  283.4 97.4 %all-to-all-start.7 = ((bf16[16,2,16,32,128]{4,3,2,1,0:T(8,128)(2,1)}), bf16[16,2,16,32,128]{4,3,2,1,0:T(8,128)(2,1)}, u32[]{:S(2)}, u32[]{:S(2)}) async-start(bf16[16,2,16,32,128]{4,3,2,1,0:T(8,128)(2,1)} %copy-done.4), calls=%async_computation.7 | async-start | bytes 8388608 | tf_op jit(solution)/shard_map/all_to_all | solution.py:319
  380.7 142.3 %all-to-all-start.1 = ((bf16[16,3,16,32,128]{4,3,2,1,0:T(8,128)(2,1)}), bf16[16,3,16,32,128]{4,3,2,1,0:T(8,128)(2,1)}, u32[]{:S(2)}, u32[]{:S(2)}) async-start(bf16[16,3,16,32,128]{4,3,2,1,0:T(8,128)(2,1)} %shard_map.78), calls=%async_computation.1 | async-start | bytes 12582912 | tf_op jit(solution)/shard_map/all_to_all | solution.py:319
  385.5 6.3 copy-start.16
  448.9 2.1 copy-start.9
  523.1 97.4 %all-to-all-start.8 = ((bf16[16,2,16,32,128]{4,3,2,1,0:T(8,128)(2,1)}), bf16[16,2,16,32,128]{4,3,2,1,0:T(8,128)(2,1)}, u32[]{:S(2)}, u32[]{:S(2)}) async-start(bf16[16,2,16,32,128]{4,3,2,1,0:T(8,128)(2,1)} %get-tuple-element.17), calls=%async_computation.8 | async-start | bytes 8388608 | tf_op jit(solution)/shard_map/all_to_all | solution.py:317
  527.8 2.2 copy-start.1
  620.4 142.3 %all-to-all-start.2 = ((bf16[16,3,16,32,128]{4,3,2,1,0:T(8,128)(2,1)}), bf16[16,3,16,32,128]{4,3,2,1,0:T(8,128)(2,1)}, u32[]{:S(2)}, u32[]{:S(2)}) async-start(bf16[16,3,16,32,128]{4,3,2,1,0:T(8,128)(2,1)} %get-tuple-element.13), calls=%async_computation.2 | async-start | bytes 12582912 | tf_op jit(solution)/shard_map/all_to_all | solution.py:317
  633.6 2.0 copy-start.6
  762.8 97.4 %all-to-all-start.9 = ((bf16[16,2,16,32,128]{4,3,2,1,0:T(8,128)(2,1)}), bf16[16,2,16,32,128]{4,3,2,1,0:T(8,128)(2,1)}, u32[]{:S(2)}, u32[]{:S(2)}) async-start(bf16[16,2,16,32,128]{4,3,2,1,0:T(8,128)(2,1)} %copy-done.6), calls=%async_computation.9 | async-start | bytes 8388608 | tf_op jit(solution)/shard_map/all_to_all | solution.py:319
  860.1 142.3 %all-to-all-start.3 = ((bf16[16,3,16,32,128]{4,3,2,1,0:T(8,128)(2,1)}), bf16[16,3,16,32,128]{4,3,2,1,0:T(8,128)(2,1)}, u32[]{:S(2)}, u32[]{:S(2)}) async-start(bf16[16,3,16,32,128]{4,3,2,1,0:T(8,128)(2,1)} %shard_map.80), calls=%async_computation.3 | async-start | bytes 12582912 | tf_op jit(solution)/shard_map/all_to_all | solution.py:319
  917.0 2.1 copy-start.10
  1002.4 97.4 %all-to-all-start.10 = ((bf16[16,2,16,32,128]{4,3,2,1,0:T(8,128)(2,1)}), bf16[16,2,16,32,128]{4,3,2,1,0:T(8,128)(2,1)}, u32[]{:S(2)}, u32[]{:S(2)}) async-start(bf16[16,2,16,32,128]{4,3,2,1,0:T(8,128)(2,1)} %get-tuple-element.19), calls=%async_computation.10 | async-start | bytes 8388608 | tf_op jit(solution)/shard_map/all_to_all | solution.py:317
  1007.1 2.2 copy-start.2
  1099.8 142.3 %all-to-all-start.4 = ((bf16[16,3,16,32,128]{4,3,2,1,0:T(8,128)(2,1)}), bf16[16,3,16,32,128]{4,3,2,1,0:T(8,128)(2,1)}, u32[]{:S(2)}, u32[]{:S(2)}) async-start(bf16[16,3,16,32,128]{4,3,2,1,0:T(8,128)(2,1)} %get-tuple-element.15), calls=%async_computation.4 | async-start | bytes 12582912 | tf_op jit(solution)/shard_map/all_to_all | solution.py:317
  1113.0 2.0 copy-start.5
  1242.1 97.4 %all-to-all-start.11 = ((bf16[16,2,16,32,128]{4,3,2,1,0:T(8,128)(2,1)}), bf16[16,2,16,32,128]{4,3,2,1,0:T(8,128)(2,1)}, u32[]{:S(2)}, u32[]{:S(2)}) async-start(bf16[16,2,16,32,128]{4,3,2,1,0:T(8,128)(2,1)} %copy-done.5), calls=%async_computation.11 | async-start | bytes 8388608 | tf_op jit(solution)/shard_map/all_to_all | solution.py:319
  1339.5 142.3 %all-to-all-start.5 = ((bf16[16,3,16,32,128]{4,3,2,1,0:T(8,128)(2,1)}), bf16[16,3,16,32,128]{4,3,2,1,0:T(8,128)(2,1)}, u32[]{:S(2)}, u32[]{:S(2)}) async-start(bf16[16,3,16,32,128]{4,3,2,1,0:T(8,128)(2,1)} %shard_map.82), calls=%async_computation.5 | async-start | bytes 12582912 | tf_op jit(solution)/shard_map/all_to_all | solution.py:319
  1390.2 1.9 copy-start.7
  1481.8 2.2 copy-start.3
  1550.4 4.0 copy-start.11
  1556.7 2.8 copy-start.8
  1559.5 2.8 copy-start.12
  1569.9 7.5 copy-start.14
